TPU v7x, 512 devices: a whole 4x4x16 slice. The times are simulated.
512 devices in a mesh: tm: 32 (over x, y, core), pitch: 16 (over z).
Axes of the slice: x: 4, y: 4, z: 16, core: 2. Of those that a mesh axis runs over, the one named last changes fastest.
Arguments:
- flow: float32 [5, 256, 32768], P(None, 'tm', 'pitch'), may hold values from -6 to 6
- speed: float32 [32768], P('pitch'), may hold values from 0.5 to 2
- rotor_face: float32 [256, 64, 5, 128], P('tm', 'pitch'), may hold values from -6 to 6
- owner: int32 [64, 1], P('pitch'), may hold values from 0 to 15; in each aligned block of 4 rows (0 to 3, 4 to 7, ...) at most 2 rows name the same one
- dest_block: int32 [64], P('pitch'), may hold values from 0 to 15
- intersection: float32 [64], P('pitch'), may hold values from 0.25 to 1
Outputs:
- residual: float32 [5, 256, 32768], P(None, 'tm', 'pitch')
- mean_flow: float32 [5, 32768], P(None, 'pitch')
Inputs may be any that keep to these rules, and one draw needn't show every extreme that they name: Among the 4 face blocks of one pitch index no owner is named more than 2 times, a bound that some block reaches.
All inputs are finite; a program needn't handle non-finite values.
Results may differ from a plain program's by a relative error of at most 0.000071.
Values sent between devices are 32-bit elements; how exact they have to be, the bound alone decides.
No kernel may reach another device: no remote copies, remote signals or barrier semaphores. Data moves between devices by JAX's collectives and lax.ppermute only.
A program may use at most 64 MiB of HBM per device.

v0:
```python
import jax
import jax.numpy as jnp
from jax import lax
from jax.sharding import PartitionSpec as P


def padded_2(cells, sides, width):
    for axis, dim in sides:
        count = lax.axis_size(axis)
        head = lax.slice_in_dim(cells, 0, width, axis=dim)
        tail = lax.slice_in_dim(cells, cells.shape[dim] - width, cells.shape[dim], axis=dim)
        cells = jnp.concatenate(
            [
                lax.ppermute(tail, axis, [(i, (i + 1) % count) for i in range(count)]),
                cells,
                lax.ppermute(head, axis, [((i + 1) % count, i) for i in range(count)]),
            ],
            axis=dim,
        )
    return cells


def spectral_matrix(rows, cols, count):
    gap = (rows[:, None] - cols[None, :]) % count
    safe = jnp.where(gap == 0, 1, gap).astype(jnp.float32)
    angle = jnp.float32(jnp.pi) * safe / count
    parity = (1 - 2 * (gap % 2)).astype(jnp.float32)
    value = jnp.float32(jnp.pi) / count * parity * jnp.cos(angle) / jnp.sin(angle)
    return jnp.where(gap == 0, jnp.float32(0.0), value)


def per_device(flow, speed, rotor_face, owner, dest_block, intersection):
    nvars, inst_dev, cells = flow.shape
    tm_count = lax.axis_size("tm")
    count = inst_dev * tm_count
    tm_index = lax.axis_index("tm")
    rows = tm_index * inst_dev + jnp.arange(inst_dev, dtype=jnp.int32)
    piece = lax.all_gather(flow, "tm", axis=1, tiled=True)
    cols = jnp.arange(piece.shape[1], dtype=jnp.int32)
    block = spectral_matrix(rows, cols, count)
    part = jnp.einsum("ts,vsc->vtc", block, piece, precision=lax.Precision.HIGHEST)
    totals = jnp.sum(piece, axis=1)
    mean_flow = totals / count
    padded = padded_2(flow, (("pitch", 2),), 1)
    convective = -speed[None, None, :] * (padded[:, :, 2:] - padded[:, :, :-2]) * 0.5
    nblocks = cells // 128
    pitch_index = lax.axis_index("pitch")
    weighted = intersection[None, :, None, None] * rotor_face
    block_ids = jnp.arange(nblocks, dtype=jnp.int32)
    target = (owner[:, 0] * nblocks + dest_block)[None, :]
    values = lax.all_gather(weighted, "pitch", axis=1, tiled=True)
    targets = lax.all_gather(target, "pitch", axis=1, tiled=True)
    hits = (targets[0][:, None] == pitch_index * nblocks + block_ids[None, :]).astype(jnp.float32)
    inject = jnp.einsum("fb,tfvj->vtbj", hits, values, precision=lax.Precision.HIGHEST)
    inject = inject.reshape(nvars, inst_dev, cells)
    residual = part + convective + inject
    return (residual, mean_flow)


def solution(mesh):
    placed = (
        P(None, "tm", "pitch"),
        P("pitch"),
        P("tm", "pitch", None, None),
        P("pitch", None),
        P("pitch"),
        P("pitch"),
    )
    return jax.shard_map(
        per_device,
        mesh=mesh,
        in_specs=placed,
        out_specs=(P(None, "tm", "pitch"), P(None, "pitch")),
        check_vma=False,
    )
```

profile of v0, /device:TPU:1, one launch (start us, length us, event | category | flops | bytes accessed | tf_op | source)
XLA Modules:
  0.0 183.6 jit_solution(16511367004041872187)
XLA Ops:
  7.2 0.0 all-gather.6.cloned.1.call-start
  7.2 1.6 copy_multiply_fusion
  8.8 0.0 all-gather.6.cloned.1.call-update
  8.8 0.0 all-gather.4.cloned.1.call-start
  8.9 0.7 all-gather.4.cloned.1.call-update
  9.6 0.8 fusion.55
  10.4 11.9 %collective-permute-start = (f32[5,8,1]{2,1,0:T(8,128)S(1)}, f32[5,8,1]{2,1,0:T(8,128)S(1)}, u32[]{:S(2)}, u32[]{:S(2)}) collective-permute-start(f32[5,8,1]{2,1,0:T(8,128)S(1)} %get-tuple-element.2), channel_id=1, source_target_pairs={{1,0},{2,1},{3,2},{4,3},{5,4},{6,5},{7,6},{8,7},{9,8},{10,9},{11,1... | collective-permute-start | bytes 488 | tf_op jit(solution)/shard_map/ppermute | solution.py:16
  22.4 1.9 %collective-permute-start.1 = (f32[5,8,1]{2,1,0:T(8,128)S(1)}, f32[5,8,1]{2,1,0:T(8,128)S(1)}, u32[]{:S(2)}, u32[]{:S(2)}) collective-permute-start(f32[5,8,1]{2,1,0:T(8,128)S(1)} %get-tuple-element.3), channel_id=1, source_target_pairs={{0,1},{1,2},{2,3},{3,4},{4,5},{5,6},{6,7},{7,8},{8,9},{9,10},{10,1... | collective-permute-start | bytes 488 | tf_op jit(solution)/shard_map/ppermute | solution.py:14
  24.3 0.7 neg.4
  25.0 1.3 dynamic-slice
  26.9 0.8 fusion.47
  27.7 15.8 %all-reduce = s32[64]{0:T(128)S(1)} all-reduce(s32[64]{0:T(128)S(1)} %fusion.47), channel_id=2, replica_groups=mesh['tm'=32,'pitch'=16] {'pitch'}, use_global_device_ids=true, to_apply=%add | all-reduce | flops 64 | bytes 512
  43.5 34.9 %all-gather.6.cloned.1.call-done = f32[8,64,5,128]{3,0,2,1:T(8,128)} async-done(((f32[8,4,5,128]{3,0,2,1:T(8,128)}), f32[8,64,5,128]{3,0,2,1:T(8,128)}) %all-gather.6.cloned.1.call-update) | async-done | bytes 1310736 | tf_op jit(solution)/shard_map/all_gather | solution.py:51
  78.4 2.0 %fusion.2 = f32[5,8,16,128]{3,2,0,1:T(8,128)S(1)} fusion(f32[8,64,5,128]{3,0,2,1:T(8,128)} %all-gather.6.cloned.1.call-done, s32[64]{0:T(128)S(1)} %all-reduce, s32[16]{0:T(128)S(1)} %iota_add_fusion), kind=kOutput, calls=%fused_computation.3 | convolution fusion | flops 62915584 | bytes 1638720 | tf_op jit(solution)/shard_map/fb,tfvj->vtbj/dot_general | solution.py:54
  80.3 0.0 copy-start
  80.4 81.3 %all-gather.4.cloned.1.call-done = f32[5,256,2048]{2,1,0:T(8,128)} async-done(((f32[5,8,2048]{2,1,0:T(8,128)}), f32[5,256,2048]{2,1,0:T(8,128)}) %all-gather.4.cloned.1.call-update) | async-done | bytes 10485776 | tf_op jit(solution)/shard_map/all_gather | solution.py:38
  161.7 4.6 %reduce_sum.9 = f32[5,2048]{1,0:T(8,128)S(1)} reduce(f32[5,256,2048]{2,1,0:T(8,128)} %all-gather.4.cloned.1.call-done, f32[]{:T(128)} %constant.49.clone.1), dimensions={1}, to_apply=%region_0.1 | reduce | flops 2611200 | bytes 10526724 | tf_op jit(solution)/shard_map/reduce_sum | solution.py:42
  166.3 0.6 broadcast_multiply_fusion
  167.0 0.0 collective-permute-done
  167.0 0.0 collective-permute-done.1
  167.0 0.0 copy-done
  167.0 9.8 %fusion.9 = f32[5,8,2048]{2,1,0:T(8,128)} fusion(f32[5,8,2048]{2,1,0:T(8,128)S(1)} %copy-done, f32[5,8,1]{2,1,0:T(8,128)S(1)} %collective-permute-done.1, f32[5,8,1]{2,1,0:T(8,128)S(1)} %collective-permute-done, f32[5,8,16,128]{3,2,0,1:T(8,128)S(1)} %fusion.2, f32[2048]{0:T(1024)S(1)} %neg.4, f32[5,256,2048]{2,1,0:T(8,128)} %all-gather.4.cloned.1.call-done, ...), kind=kOutput, calls=%fused_computation.9 | convolution fusion | flops 252301312 | bytes 11477344 | tf_op jit(solution)/shard_map/ts,vsc->vtc/dot_general | solution.py:41
  (3 shorter events, 0.0 us)
Async XLA Ops:
  7.2 71.2 %all-gather.6.cloned.1.call-start = ((), (), s32[]{:S(2)}) async-start(), calls=%async_computation.1 | async-start | bytes 1392640 | tf_op jit(solution)/shard_map/all_gather | solution.py:51
  8.8 152.9 %all-gather.4.cloned.1.call-start = ((), (), s32[]{:S(2)}) async-start(), calls=%async_computation | async-start | bytes 10813440 | tf_op jit(solution)/shard_map/all_gather | solution.py:38
  10.4 156.6 %collective-permute-start = (f32[5,8,1]{2,1,0:T(8,128)S(1)}, f32[5,8,1]{2,1,0:T(8,128)S(1)}, u32[]{:S(2)}, u32[]{:S(2)}) collective-permute-start(f32[5,8,1]{2,1,0:T(8,128)S(1)} %get-tuple-element.2), channel_id=1, source_target_pairs={{1,0},{2,1},{3,2},{4,3},{5,4},{6,5},{7,6},{8,7},{9,8},{10,9},{11,1... | collective-permute-start | bytes 488 | tf_op jit(solution)/shard_map/ppermute | solution.py:16
  22.4 144.6 %collective-permute-start.1 = (f32[5,8,1]{2,1,0:T(8,128)S(1)}, f32[5,8,1]{2,1,0:T(8,128)S(1)}, u32[]{:S(2)}, u32[]{:S(2)}) collective-permute-start(f32[5,8,1]{2,1,0:T(8,128)S(1)} %get-tuple-element.3), channel_id=1, source_target_pairs={{0,1},{1,2},{2,3},{3,4},{4,5},{5,6},{6,7},{7,8},{8,9},{9,10},{10,1... | collective-permute-start | bytes 488 | tf_op jit(solution)/shard_map/ppermute | solution.py:14
  80.3 86.6 %copy-start = (f32[5,8,2048]{2,1,0:T(8,128)S(1)}, f32[5,8,2048]{2,1,0:T(8,128)}, u32[]{:S(2)}) copy-start(f32[5,8,2048]{2,1,0:T(8,128)} %param.6) | copy-start | bytes 983044
Sparse Core Ops, SparseCore 0:
  10.7 67.6 all-gather.5
  81.6 80.0 all-gather.3
where the time goes:
time: 184 us
  waiting for transfers between devices  117 us (64%)
  blocking collectives  15.8 us (9%)
  between operations  14.8 us (8%)
  starting transfers between devices  13.9 us (8%)
  matrix products  11.8 us (6%)
  other arithmetic  8.35 us (5%)
  local copies, waits for them, and re-layouts  2.09 us (1%)
    all_gather x1, waiting for transfers between devices, per_device(): piece = lax.all_gather(flow, 'tm', axis=1, tiled=True)  81.3 us
    all_gather x1, waiting for transfers between devices, per_device(): values = lax.all_gather(weighted, 'pitch', axis=1, tiled=True)  34.9 us
    unnamed x1, blocking collectives  15.8 us
    ppermute x1, starting transfers between devices, padded_2(): lax.ppermute(head, axis, [((i + 1) % count, i) for i in range(count)])  11.9 us
    dot_general x1, matrix products, per_device(): jnp.einsum('ts,vsc->vtc', block, piece, precision=lax.Precision.HIGHEST)  9.81 us
    reduce_sum x1, other arithmetic, per_device(): totals = jnp.sum(piece, axis=1)  4.64 us
  transfers between devices with their start and end apart: 4, of which 2 were waited for; matrix products, arithmetic and copies ran while one was open for 6% of the time, Pallas kernels for 0%

commit v1 on v0

v1 whole, which is shorter than its diff:
```python
import jax
import jax.numpy as jnp
from jax import lax
from jax.experimental import pallas as pl
from jax.experimental.pallas import tpu as pltpu
from jax.sharding import PartitionSpec as P

LANES = 128
ROWS = 8
META = 8
OWNER_AT, DEST_AT = 16, 24
VMEM = 32 * 1024 * 1024
NEAR = (1, -1)
RELAYED = (3, -3, 6, -6)
DIRECT = (8,)


def vmem():
    return pl.BlockSpec(memory_space=pltpu.VMEM)


def smem():
    return pl.BlockSpec(memory_space=pltpu.SMEM)


def call(body, outs, in_specs, scratch=(), flops=0, moved=0):
    return pl.pallas_call(
        body,
        out_shape=outs,
        in_specs=in_specs,
        out_specs=jax.tree.map(lambda _: vmem(), outs),
        scratch_shapes=list(scratch),
        compiler_params=pltpu.CompilerParams(vmem_limit_bytes=VMEM),
        cost_estimate=pl.CostEstimate(flops=flops, bytes_accessed=moved, transcendentals=0),
    )


def f32(*shape):
    return jax.ShapeDtypeStruct(shape, jnp.float32)


def cells_out_kernel(flow_ref, out_ref):
    nvars, _, cells = flow_ref.shape
    per = cells // LANES
    tiles = nvars * per
    row = lax.broadcasted_iota(jnp.int32, (ROWS, LANES), 0)
    sums = None
    for m in range(tiles):
        v, c = divmod(m, per)
        tile = flow_ref[v, :, c * LANES : (c + 1) * LANES]
        out_ref[m * ROWS : (m + 1) * ROWS, :] = tile
        total = jnp.sum(tile, axis=0, keepdims=True)
        total = jnp.broadcast_to(total, (ROWS, LANES))
        sums = total if m % ROWS == 0 else jnp.where(row == m % ROWS, total, sums)
        if m % ROWS == ROWS - 1:
            q = tiles + m // ROWS
            out_ref[q * ROWS : (q + 1) * ROWS, :] = sums
    used = (tiles + tiles // ROWS) * ROWS
    rest = out_ref.shape[0] - used
    out_ref[used:, :] = jnp.zeros((rest, LANES), jnp.float32)


def weigh_kernel(owner_ref, dest_ref, weight_ref, flow_ref, rotor_ref, *out_refs):
    mine_ref, direct_refs = out_refs[0], out_refs[1:]
    nvars, _, cells = flow_ref.shape
    faces = weight_ref.shape[0]
    block = nvars * ROWS
    me = lax.axis_index("pitch")
    count = lax.axis_size("pitch")
    lane = lax.broadcasted_iota(jnp.int32, (ROWS, LANES), 1)
    meta = jnp.zeros((ROWS, LANES), jnp.float32)
    for v in range(nvars):
        tail = pltpu.roll(flow_ref[v, :, cells - LANES :], v + 1, 1)
        head = pltpu.roll(flow_ref[v, :, :LANES], nvars + v, 1)
        meta = jnp.where(lane == v, tail, meta)
        meta = jnp.where(lane == nvars + v, head, meta)
    for f in range(faces):
        meta = jnp.where(lane == OWNER_AT + f, owner_ref[f].astype(jnp.float32), meta)
        meta = jnp.where(lane == DEST_AT + f, dest_ref[f].astype(jnp.float32), meta)
        for v in range(nvars):
            rows = rotor_ref[pl.ds(v * faces + f, ROWS, stride=nvars * faces), :]
            at = f * block + v * ROWS
            mine_ref[at : at + ROWS, :] = weight_ref[f] * rows
    mine_ref[faces * block :, :] = meta
    for offset, out_ref in zip(DIRECT, direct_refs):
        route(
            [(mine_ref, f * block, owner_ref[f], dest_ref[f]) for f in range(faces)],
            lax.rem(me + (offset + count), count),
            block,
            out_ref,
        )


def route(items, target, block, out_ref):
    lane = lax.broadcasted_iota(jnp.int32, (META, LANES), 1)
    slots = (out_ref.shape[0] - META) // block
    meta = jnp.full((META, LANES), -1.0, jnp.float32)
    used = jnp.int32(0)
    for ref, at, owner, dest in items:
        hit = owner == target

        @pl.when(hit)
        def _(ref=ref, at=at, used=used):
            to = pl.multiple_of(used * block, block)
            out_ref[pl.ds(to, block), :] = ref[at : at + block, :]

        where = jnp.where(hit, DEST_AT + used, -1)
        meta = jnp.where(lane == where, dest.astype(jnp.float32), meta)
        used = used + hit.astype(jnp.int32)
    out_ref[slots * block :, :] = meta


def fetch_ids(refs, ids_ref, sems):
    copies = [
        pltpu.make_async_copy(ref.at[pl.ds(ref.shape[0] - META, META), :], ids_ref.at[i], sems.at[i])
        for i, ref in enumerate(refs)
    ]
    for copy in copies:
        copy.start()

    def wait():
        for copy in copies:
            copy.wait()

    return wait


def id_scratch(groups):
    return [pltpu.SMEM((groups, META, LANES), jnp.float32), pltpu.SemaphoreType.DMA((groups,))]


def received(faces, block, refs, ids_ref):
    items = []
    for i, ref in enumerate(refs):
        for f in range(faces):
            ids = [ids_ref[i, 0, at + f].astype(jnp.int32) for at in (OWNER_AT, DEST_AT)]
            items.append((ref, f * block, *ids))
    return items


def relay_kernel(owner_ref, dest_ref, mine_ref, below_ref, above_ref, *rest):
    out_refs, ids_ref, sems = rest[:-2], rest[-2], rest[-1]
    wait = fetch_ids((below_ref, above_ref), ids_ref, sems)
    faces = owner_ref.shape[0]
    block = (mine_ref.shape[0] - META) // faces
    me = lax.axis_index("pitch")
    count = lax.axis_size("pitch")
    items = []
    for f in range(faces):
        items.append((mine_ref, f * block, owner_ref[f], dest_ref[f]))
    wait()
    items += received(faces, block, (below_ref, above_ref), ids_ref)
    for offset, out_ref in zip(RELAYED, out_refs):
        route(items, lax.rem(me + (offset + count), count), block, out_ref)


def add_block(out_ref, ref, at, dest):
    nvars = out_ref.shape[0]
    to = pl.ds(pl.multiple_of(dest * LANES, LANES), LANES)
    for v in range(nvars):
        out_ref[v, :, to] += ref[at + v * ROWS : at + (v + 1) * ROWS, :]


def base_kernel(owner_ref, dest_ref, flow_ref, speed_ref, mine_ref, below_ref, above_ref, out_ref, ids_ref, sems):
    wait = fetch_ids((below_ref, above_ref), ids_ref, sems)
    nvars, _, cells = flow_ref.shape
    faces = owner_ref.shape[0]
    block = nvars * ROWS
    per = cells // LANES
    me = lax.axis_index("pitch")
    lane = lax.broadcasted_iota(jnp.int32, (ROWS, LANES), 1)
    before, after = below_ref[faces * block :, :], above_ref[faces * block :, :]
    for v in range(nvars):
        left_edge = pltpu.roll(before, (LANES - v) % LANES, 1)
        right_edge = pltpu.roll(after, LANES - 1 - nvars - v, 1)
        tiles = [flow_ref[v, :, c * LANES : (c + 1) * LANES] for c in range(per)]
        downs = [pltpu.roll(tile, 1, 1) for tile in tiles]
        ups = [pltpu.roll(tile, LANES - 1, 1) for tile in tiles]
        for c in range(per):
            down = jnp.where(lane == 0, left_edge if c == 0 else downs[c - 1], downs[c])
            up = jnp.where(lane == LANES - 1, right_edge if c == per - 1 else ups[c + 1], ups[c])
            speed = speed_ref[c : c + 1, :]
            out_ref[v, :, c * LANES : (c + 1) * LANES] = -speed * (up - down) * 0.5
    items = [(mine_ref, f * block, owner_ref[f], dest_ref[f]) for f in range(faces)]
    wait()
    items += received(faces, block, (below_ref, above_ref), ids_ref)
    for ref, at, owner, dest in items:

        @pl.when(owner == me)
        def _(ref=ref, at=at, dest=dest):
            add_block(out_ref, ref, at, dest)


def spectral_kernel(matrix_ref, cells_ref, out_ref, *, first_mean, last_mean):
    count = matrix_ref.shape[0]
    devs = count // ROWS
    slots = cells_ref.shape[0] // count
    me = lax.axis_index("tm")
    got = cells_ref[...].reshape(devs, slots, ROWS, LANES)
    columns = jnp.concatenate([got[:, k].reshape(count, LANES) for k in range(slots)], axis=1)
    product = jnp.dot(matrix_ref[...], columns, precision=lax.Precision.HIGHEST, preferred_element_type=jnp.float32)
    for k in range(slots):
        tile = me * slots + k
        is_mean = jnp.logical_and(tile >= first_mean, tile < last_mean)
        mean = jnp.sum(got[:, k], axis=0) / count
        for d in range(devs):
            part = product[d * ROWS : (d + 1) * ROWS, k * LANES : (k + 1) * LANES]
            at = (d * slots + k) * ROWS
            out_ref[at : at + ROWS, :] = jnp.where(is_mean, mean, part)


def finish_kernel(*refs):
    base_ref, cells_ref, blocks = refs[0], refs[1], refs[2:-4]
    out_ref, mean_ref, ids_ref, sems = refs[-4:]
    wait = fetch_ids(blocks, ids_ref, sems)
    nvars, _, cells = out_ref.shape
    block = nvars * ROWS
    per = cells // LANES
    for m in range(nvars * per):
        v, c = divmod(m, per)
        at = slice(c * LANES, (c + 1) * LANES)
        out_ref[v, :, at] = cells_ref[m * ROWS : (m + 1) * ROWS, :] + base_ref[v, :, at]
        row = nvars * per * ROWS + m
        mean_ref[v : v + 1, at] = cells_ref[row : row + 1, :]
    wait()
    for i, ref in enumerate(blocks):
        for slot in range((ref.shape[0] - META) // block):
            dest = ids_ref[i, 0, DEST_AT + slot].astype(jnp.int32)

            @pl.when(dest >= 0)
            def _(ref=ref, slot=slot, dest=dest):
                add_block(out_ref, ref, slot * block, dest)


def spectral_matrix(count):
    index = jnp.arange(count, dtype=jnp.int32)
    gap = (index[:, None] - index[None, :]) % count
    safe = jnp.where(gap == 0, 1, gap).astype(jnp.float32)
    angle = jnp.float32(jnp.pi) * safe / count
    parity = (1 - 2 * (gap % 2)).astype(jnp.float32)
    value = jnp.float32(jnp.pi) / count * parity * jnp.cos(angle) / jnp.sin(angle)
    return jnp.where(gap == 0, jnp.float32(0.0), value)


def shifted(array, by):
    count = lax.axis_size("pitch")
    return lax.ppermute(array, "pitch", [(i, (i + by) % count) for i in range(count)])


def per_device(flow, speed, rotor_face, owner, dest_block, intersection):
    nvars, inst, cells = flow.shape
    faces = rotor_face.shape[1]
    devs = lax.axis_size("tm")
    count = inst * devs
    block = nvars * inst
    tiles = nvars * cells // LANES
    slots = -(-(tiles + tiles // ROWS) // devs)
    owner = owner.reshape(faces)
    rotor = jnp.transpose(rotor_face, (0, 2, 1, 3)).reshape(inst * nvars * faces, LANES)
    speed = speed.reshape(cells // LANES, LANES)

    packed = call(cells_out_kernel, f32(devs * slots * ROWS, LANES), [vmem()], moved=700_000)(flow)
    mine, *direct = call(
        weigh_kernel,
        [f32(faces * block + META, LANES)] + [f32(2 * block + META, LANES) for _ in DIRECT],
        [smem(), smem(), smem(), vmem(), vmem()],
        moved=600_000,
    )(owner, dest_block, intersection, flow, rotor)
    by_cell = lax.all_to_all(packed, "tm", 0, 0, tiled=True)
    below, above = shifted(mine, 1), shifted(mine, -1)
    relays = call(
        relay_kernel,
        [f32(6 * block + META, LANES) for _ in RELAYED],
        [smem(), smem(), vmem(), vmem(), vmem()],
        id_scratch(2),
        moved=700_000,
    )(owner, dest_block, mine, below, above)
    by_cell, relays = lax.optimization_barrier((by_cell, relays))
    sent = [shifted(a, by) for a, by in zip(relays, RELAYED)]
    sent += [shifted(a, by) for a, by in zip(direct, DIRECT)]
    base = call(
        base_kernel,
        f32(nvars, inst, cells),
        [smem(), smem(), vmem(), vmem(), vmem(), vmem(), vmem()],
        id_scratch(2),
        moved=900_000,
    )(owner, dest_block, flow, speed, mine, below, above)

    def spectral(matrix_ref, cells_ref, out_ref):
        spectral_kernel(matrix_ref, cells_ref, out_ref, first_mean=tiles, last_mean=tiles + tiles // ROWS)

    product = call(spectral, f32(devs * slots * ROWS, LANES), [vmem(), vmem()], flops=6 * 2 * count * count * slots * LANES, moved=1_000_000)(
        spectral_matrix(count), by_cell
    )
    by_time = lax.all_to_all(product, "tm", 0, 0, tiled=True)
    residual, mean_flow = call(
        finish_kernel,
        (f32(nvars, inst, cells), f32(nvars, cells)),
        [vmem()] * (2 + len(sent)),
        id_scratch(len(sent)),
        moved=1_500_000,
    )(base, by_time, *sent)
    return residual, mean_flow


def solution(mesh):
    placed = (
        P(None, "tm", "pitch"),
        P("pitch"),
        P("tm", "pitch", None, None),
        P("pitch", None),
        P("pitch"),
        P("pitch"),
    )
    return jax.shard_map(
        per_device,
        mesh=mesh,
        in_specs=placed,
        out_specs=(P(None, "tm", "pitch"), P(None, "pitch")),
        check_vma=False,
    )
```

time: 184 us -> 84.7 us (0.46)
  the two profiles are of different devices: /device:TPU:1 before, /device:TPU:67 now
where the time goes in v1:
time: 84.7 us; the launch traced here: 84.2 us
  starting transfers between devices  52.7 us (62%)
  waiting for transfers between devices  20.1 us (24%)
  Pallas kernels  7.82 us (9%)
  local copies, waits for them, and re-layouts  1.62 us (2%)
  other arithmetic  1.17 us (1%)
    ppermute x7, starting transfers between devices, shifted(): lax.ppermute(array, 'pitch', [(i, (i + by) % count) for i in range(count)])  36.3 us
    ppermute x7, waiting for transfers between devices, shifted(): lax.ppermute(array, 'pitch', [(i, (i + by) % count) for i in range(count)])  20 us
    all_to_all x1, starting transfers between devices, per_device(): by_time = lax.all_to_all(product, 'tm', 0, 0, tiled=True)  8.34 us
    all_to_all x1, starting transfers between devices, per_device(): by_cell = lax.all_to_all(packed, 'tm', 0, 0, tiled=True)  8.07 us
    pallas_call x1, Pallas kernels, per_device(): call(finish_kernel, (f32(nvars, inst, cells), f32(nvars, cells)), [vmem()...  1.94 us
  transfers between devices with their start and end apart: 9, of which 4 were waited for; matrix products, arithmetic and copies ran while one was open for 1% of the time, Pallas kernels for 4%

profile of v1, /device:TPU:67, one launch (start us, length us, event | category | flops | bytes accessed | tf_op | source)
XLA Modules:
  0.0 84.2 jit_solution(7896991862792396632)
XLA Ops:
  0.6 0.0 copy-start
  0.6 1.0 %copy-done = f32[5,8,2048]{2,1,0:T(8,128)S(1)} copy-done((f32[5,8,2048]{2,1,0:T(8,128)S(1)}, f32[5,8,2048]{2,1,0:T(8,128)}, u32[]{:S(2)}) %copy-start) | copy-done | bytes 327704
  1.6 0.8 shard_map.79
  2.4 8.1 %all-to-all-start = ((f32[32,24,128]{2,1,0:T(8,128)}), f32[32,24,128]{2,1,0:T(8,128)S(1)}, u32[]{:S(2)}, u32[]{:S(2)}) async-start(f32[32,24,128]{2,1,0:T(8,128)} %bitcast.4), calls=%async_computation | async-start | bytes 786432 | tf_op jit(solution)/shard_map/all_to_all | solution.py:269
  10.5 0.0 copy-start.4
  10.5 0.0 copy-start.5
  10.5 0.0 copy-start.6
  10.6 0.6 copy-done.4
  11.2 0.0 copy-done.5
  11.2 0.0 copy-done.6
  11.2 0.6 shard_map.77
  11.9 3.5 %collective-permute-start = (f32[168,128]{1,0:T(8,128)S(1)}, f32[168,128]{1,0:T(8,128)S(1)}, u32[]{:S(2)}, u32[]{:S(2)}) collective-permute-start(f32[168,128]{1,0:T(8,128)S(1)} %get-tuple-element.13.mine_ref), channel_id=1, source_target_pairs={{0,1},{1,2},{2,3},{3,4},{4,5},{5,6},{6,7},{7,8},{8,9},{9,10},{10,1... | collective-permute-start | bytes 258056 | tf_op jit(solution)/shard_map/ppermute | solution.py:247
  15.4 1.9 %collective-permute-start.1 = (f32[168,128]{1,0:T(8,128)S(1)}, f32[168,128]{1,0:T(8,128)S(1)}, u32[]{:S(2)}, u32[]{:S(2)}) collective-permute-start(f32[168,128]{1,0:T(8,128)S(1)} %get-tuple-element.13.mine_ref), channel_id=1, source_target_pairs={{0,15},{1,0},{2,1},{3,2},{4,3},{5,4},{6,5},{7,6},{8,7},{9,8},{10,9... | collective-permute-start | bytes 258056 | tf_op jit(solution)/shard_map/ppermute | solution.py:247
  17.3 1.2 %compare_select_fusion.matrix_ref = f32[256,256]{1,0:T(8,128)S(1)} fusion(), kind=kLoop, calls=%fused_computation.6 | loop fusion | flops 2228224 | bytes 262144 | tf_op jit(solution)/shard_map/jit(_where)/select_n | solution.py:242
  18.5 0.0 collective-permute-done.below_ref
  18.5 3.9 %collective-permute-done.1.above_ref = f32[168,128]{1,0:T(8,128)S(1)} collective-permute-done((f32[168,128]{1,0:T(8,128)S(1)}, f32[168,128]{1,0:T(8,128)S(1)}, u32[]{:S(2)}, u32[]{:S(2)}) %collective-permute-start.1) | collective-permute-done | bytes 86048 | tf_op jit(solution)/shard_map/ppermute | solution.py:247
  22.5 1.6 %shard_map.80 = (f32[248,128]{1,0:T(8,128)S(1)}, f32[248,128]{1,0:T(8,128)S(1)}, f32[248,128]{1,0:T(8,128)S(1)}, f32[248,128]{1,0:T(8,128)S(1)}) custom-call(s32[4]{0:T(128)S(1)} %bitcast.14, s32[4]{0:T(128)S(1)} %copy-done.5, f32[168,128]{1,0:T(8,128)S(1)} %get-tuple-element.13.mine_ref, f32[168,128]{1,0:T(8,128)S(1)} %collective-permute-done.below_ref, ...), custom_call_target="tpu_custom_call" | custom-call | bytes 700000 | tf_op jit(solution)/shard_map/pallas_call | solution.py:271
  24.1 0.0 all-to-all-done
  24.1 1.4 %shard_map.81 = f32[768,128]{1,0:T(8,128)} custom-call(f32[256,256]{1,0:T(8,128)S(1)} %compare_select_fusion.matrix_ref, f32[768,128]{1,0:T(8,128)S(1)} %bitcast.10), custom_call_target="tpu_custom_call" | custom-call | flops 301989888 | bytes 1000000 | tf_op jit(solution)/shard_map/pallas_call | solution.py:292
  25.4 8.3 %all-to-all-start.1 = ((f32[32,24,128]{2,1,0:T(8,128)}), f32[32,24,128]{2,1,0:T(8,128)S(1)}, u32[]{:S(2)}, u32[]{:S(2)}) async-start(f32[32,24,128]{2,1,0:T(8,128)} %bitcast.6), calls=%async_computation.1 | async-start | bytes 786432 | tf_op jit(solution)/shard_map/all_to_all | solution.py:295
  33.8 6.3 %collective-permute-start.2 = (f32[248,128]{1,0:T(8,128)S(1)}, f32[248,128]{1,0:T(8,128)S(1)}, u32[]{:S(2)}, u32[]{:S(2)}) collective-permute-start(f32[248,128]{1,0:T(8,128)S(1)} %get-tuple-element.19), channel_id=1, source_target_pairs={{0,3},{1,4},{2,5},{3,6},{4,7},{5,8},{6,9},{7,10},{8,11},{9,12},{10... | collective-permute-start | bytes 380936 | tf_op jit(solution)/shard_map/ppermute | solution.py:247
  40.0 4.1 %collective-permute-start.3 = (f32[248,128]{1,0:T(8,128)S(1)}, f32[248,128]{1,0:T(8,128)S(1)}, u32[]{:S(2)}, u32[]{:S(2)}) collective-permute-start(f32[248,128]{1,0:T(8,128)S(1)} %get-tuple-element.20), channel_id=1, source_target_pairs={{0,13},{1,14},{2,15},{3,0},{4,1},{5,2},{6,3},{7,4},{8,5},{9,6},{10... | collective-permute-start | bytes 380936 | tf_op jit(solution)/shard_map/ppermute | solution.py:247
  44.1 8.6 %collective-permute-start.4 = (f32[248,128]{1,0:T(8,128)S(1)}, f32[248,128]{1,0:T(8,128)S(1)}, u32[]{:S(2)}, u32[]{:S(2)}) collective-permute-start(f32[248,128]{1,0:T(8,128)S(1)} %get-tuple-element.21), channel_id=1, source_target_pairs={{0,6},{1,7},{2,8},{3,9},{4,10},{5,11},{6,12},{7,13},{8,14},{9,15},... | collective-permute-start | bytes 380936 | tf_op jit(solution)/shard_map/ppermute | solution.py:247
  52.7 2.4 %collective-permute-start.5 = (f32[248,128]{1,0:T(8,128)S(1)}, f32[248,128]{1,0:T(8,128)S(1)}, u32[]{:S(2)}, u32[]{:S(2)}) collective-permute-start(f32[248,128]{1,0:T(8,128)S(1)} %get-tuple-element.22), channel_id=1, source_target_pairs={{0,10},{1,11},{2,12},{3,13},{4,14},{5,15},{6,0},{7,1},{8,2},{9,3},... | collective-permute-start | bytes 380936 | tf_op jit(solution)/shard_map/ppermute | solution.py:247
  55.1 9.5 %collective-permute-start.6 = (f32[88,128]{1,0:T(8,128)S(1)}, f32[88,128]{1,0:T(8,128)S(1)}, u32[]{:S(2)}, u32[]{:S(2)}) collective-permute-start(f32[88,128]{1,0:T(8,128)S(1)} %get-tuple-element.23), channel_id=1, source_target_pairs={{0,8},{1,9},{2,10},{3,11},{4,12},{5,13},{6,14},{7,15},{8,0},{9,1},... | collective-permute-start | bytes 135176 | tf_op jit(solution)/shard_map/ppermute | solution.py:247
  64.6 1.5 %shard_map.78.refs_0_ = f32[5,8,2048]{2,1,0:T(8,128)S(1)} custom-call(s32[4]{0:T(128)S(1)} %bitcast.15, s32[4]{0:T(128)S(1)} %copy-done.5, f32[5,8,2048]{2,1,0:T(8,128)S(1)} %copy-done.1, f32[16,128]{1,0:T(8,128)S(1)} %bitcast.12, f32[168,128]{1,0:T(8,128)S(1)} %get-tuple-element.13.mine_ref, f32[168,128]{1,0:T(8,128)S(1)} %collective-permute-done.below_ref, ...), custom_call_target="tpu_custom_call" | custom-call | bytes 900000 | tf_op jit(solution)/shard_map/pallas_call | solution.py:281
  66.1 4.4 %collective-permute-done.6.refs_6_ = f32[88,128]{1,0:T(8,128)S(1)} collective-permute-done((f32[88,128]{1,0:T(8,128)S(1)}, f32[88,128]{1,0:T(8,128)S(1)}, u32[]{:S(2)}, u32[]{:S(2)}) %collective-permute-start.6) | collective-permute-done | bytes 45088 | tf_op jit(solution)/shard_map/ppermute | solution.py:247
  70.5 0.0 collective-permute-done.2.refs_2_
  70.5 1.8 %collective-permute-done.4.refs_4_ = f32[248,128]{1,0:T(8,128)S(1)} collective-permute-done((f32[248,128]{1,0:T(8,128)S(1)}, f32[248,128]{1,0:T(8,128)S(1)}, u32[]{:S(2)}, u32[]{:S(2)}) %collective-permute-start.4) | collective-permute-done | bytes 127008 | tf_op jit(solution)/shard_map/ppermute | solution.py:247
  72.3 9.9 %collective-permute-done.5.refs_5_ = f32[248,128]{1,0:T(8,128)S(1)} collective-permute-done((f32[248,128]{1,0:T(8,128)S(1)}, f32[248,128]{1,0:T(8,128)S(1)}, u32[]{:S(2)}, u32[]{:S(2)}) %collective-permute-start.5) | collective-permute-done | bytes 127008 | tf_op jit(solution)/shard_map/ppermute | solution.py:247
  82.2 0.0 all-to-all-done.1
  82.2 1.9 %shard_map.82 = (f32[5,8,2048]{2,1,0:T(8,128)}, f32[5,2048]{1,0:T(8,128)}) custom-call(f32[5,8,2048]{2,1,0:T(8,128)S(1)} %shard_map.78.refs_0_, f32[768,128]{1,0:T(8,128)S(1)} %bitcast.9, f32[248,128]{1,0:T(8,128)S(1)} %collective-permute-done.2.refs_2_, f32[248,128]{1,0:T(8,128)S(1)} %collective-permute-done.3.refs_3_, ...), custom_call_target="tpu_custom_call" | custom-call | bytes 1500000 | tf_op jit(solution)/shard_map/pallas_call | solution.py:296
  (7 shorter events, 0.0 us)
Async XLA Ops:
  0.6 1.0 %copy-start = (f32[5,8,2048]{2,1,0:T(8,128)S(1)}, f32[5,8,2048]{2,1,0:T(8,128)}, u32[]{:S(2)}) copy-start(f32[5,8,2048]{2,1,0:T(8,128)} %flow_ref.5) | copy-start | bytes 983044
  2.4 8.1 %copy-start.1 = (f32[5,8,2048]{2,1,0:T(8,128)S(1)}, f32[5,8,2048]{2,1,0:T(8,128)}, u32[]{:S(2)}) copy-start(f32[5,8,2048]{2,1,0:T(8,128)} %flow_ref.5) | copy-start | bytes 983044
  2.4 8.1 %copy-start.2 = (f32[8,4,5,128]{3,1,2,0:T(4,128)S(1)}, f32[8,4,5,128]{3,1,2,0:T(4,128)}, u32[]{:S(2)}) copy-start(f32[8,4,5,128]{3,1,2,0:T(4,128)} %param.8) | copy-start | bytes 245764
  2.4 21.6 %all-to-all-start = ((f32[32,24,128]{2,1,0:T(8,128)}), f32[32,24,128]{2,1,0:T(8,128)S(1)}, u32[]{:S(2)}, u32[]{:S(2)}) async-start(f32[32,24,128]{2,1,0:T(8,128)} %bitcast.4), calls=%async_computation | async-start | bytes 786432 | tf_op jit(solution)/shard_map/all_to_all | solution.py:269
  10.5 0.7 copy-start.4
  10.5 0.7 copy-start.5
  10.5 0.7 copy-start.6
  11.9 6.7 %collective-permute-start = (f32[168,128]{1,0:T(8,128)S(1)}, f32[168,128]{1,0:T(8,128)S(1)}, u32[]{:S(2)}, u32[]{:S(2)}) collective-permute-start(f32[168,128]{1,0:T(8,128)S(1)} %get-tuple-element.13.mine_ref), channel_id=1, source_target_pairs={{0,1},{1,2},{2,3},{3,4},{4,5},{5,6},{6,7},{7,8},{8,9},{9,10},{10,1... | collective-permute-start | bytes 258056 | tf_op jit(solution)/shard_map/ppermute | solution.py:247
  15.4 7.0 %collective-permute-start.1 = (f32[168,128]{1,0:T(8,128)S(1)}, f32[168,128]{1,0:T(8,128)S(1)}, u32[]{:S(2)}, u32[]{:S(2)}) collective-permute-start(f32[168,128]{1,0:T(8,128)S(1)} %get-tuple-element.13.mine_ref), channel_id=1, source_target_pairs={{0,15},{1,0},{2,1},{3,2},{4,3},{5,4},{6,5},{7,6},{8,7},{9,8},{10,9... | collective-permute-start | bytes 258056 | tf_op jit(solution)/shard_map/ppermute | solution.py:247
  25.4 39.2 %copy-start.3 = (f32[2048]{0:T(1024)S(1)}, f32[2048]{0:T(1024)}, u32[]{:S(2)}) copy-start(f32[2048]{0:T(1024)} %param.7) | copy-start | bytes 24580
  25.4 56.8 %all-to-all-start.1 = ((f32[32,24,128]{2,1,0:T(8,128)}), f32[32,24,128]{2,1,0:T(8,128)S(1)}, u32[]{:S(2)}, u32[]{:S(2)}) async-start(f32[32,24,128]{2,1,0:T(8,128)} %bitcast.6), calls=%async_computation.1 | async-start | bytes 786432 | tf_op jit(solution)/shard_map/all_to_all | solution.py:295
  33.8 36.7 %collective-permute-start.2 = (f32[248,128]{1,0:T(8,128)S(1)}, f32[248,128]{1,0:T(8,128)S(1)}, u32[]{:S(2)}, u32[]{:S(2)}) collective-permute-start(f32[248,128]{1,0:T(8,128)S(1)} %get-tuple-element.19), channel_id=1, source_target_pairs={{0,3},{1,4},{2,5},{3,6},{4,7},{5,8},{6,9},{7,10},{8,11},{9,12},{10... | collective-permute-start | bytes 380936 | tf_op jit(solution)/shard_map/ppermute | solution.py:247
  40.0 30.5 %collective-permute-start.3 = (f32[248,128]{1,0:T(8,128)S(1)}, f32[248,128]{1,0:T(8,128)S(1)}, u32[]{:S(2)}, u32[]{:S(2)}) collective-permute-start(f32[248,128]{1,0:T(8,128)S(1)} %get-tuple-element.20), channel_id=1, source_target_pairs={{0,13},{1,14},{2,15},{3,0},{4,1},{5,2},{6,3},{7,4},{8,5},{9,6},{10... | collective-permute-start | bytes 380936 | tf_op jit(solution)/shard_map/ppermute | solution.py:247
  44.1 28.2 %collective-permute-start.4 = (f32[248,128]{1,0:T(8,128)S(1)}, f32[248,128]{1,0:T(8,128)S(1)}, u32[]{:S(2)}, u32[]{:S(2)}) collective-permute-start(f32[248,128]{1,0:T(8,128)S(1)} %get-tuple-element.21), channel_id=1, source_target_pairs={{0,6},{1,7},{2,8},{3,9},{4,10},{5,11},{6,12},{7,13},{8,14},{9,15},... | collective-permute-start | bytes 380936 | tf_op jit(solution)/shard_map/ppermute | solution.py:247
  52.7 29.5 %collective-permute-start.5 = (f32[248,128]{1,0:T(8,128)S(1)}, f32[248,128]{1,0:T(8,128)S(1)}, u32[]{:S(2)}, u32[]{:S(2)}) collective-permute-start(f32[248,128]{1,0:T(8,128)S(1)} %get-tuple-element.22), channel_id=1, source_target_pairs={{0,10},{1,11},{2,12},{3,13},{4,14},{5,15},{6,0},{7,1},{8,2},{9,3},... | collective-permute-start | bytes 380936 | tf_op jit(solution)/shard_map/ppermute | solution.py:247
  55.1 15.4 %collective-permute-start.6 = (f32[88,128]{1,0:T(8,128)S(1)}, f32[88,128]{1,0:T(8,128)S(1)}, u32[]{:S(2)}, u32[]{:S(2)}) collective-permute-start(f32[88,128]{1,0:T(8,128)S(1)} %get-tuple-element.23), channel_id=1, source_target_pairs={{0,8},{1,9},{2,10},{3,11},{4,12},{5,13},{6,14},{7,15},{8,0},{9,1},... | collective-permute-start | bytes 135176 | tf_op jit(solution)/shard_map/ppermute | solution.py:247

commit v2 on v1

--- a/solution.py
+++ b/solution.py
@@ -1,3 +1,5 @@
+import functools
+
 import jax
 import jax.numpy as jnp
 from jax import lax
@@ -10,9 +12,8 @@
 META = 8
 OWNER_AT, DEST_AT = 16, 24
 VMEM = 32 * 1024 * 1024
-NEAR = (1, -1)
-RELAYED = (3, -3, 6, -6)
-DIRECT = (8,)
+CAP = 2
+CLASSES = 4
 
 
 def vmem():
@@ -60,13 +61,10 @@
     out_ref[used:, :] = jnp.zeros((rest, LANES), jnp.float32)
 
 
-def weigh_kernel(owner_ref, dest_ref, weight_ref, flow_ref, rotor_ref, *out_refs):
-    mine_ref, direct_refs = out_refs[0], out_refs[1:]
+def weigh_kernel(owner_ref, dest_ref, weight_ref, flow_ref, rotor_ref, mine_ref):
     nvars, _, cells = flow_ref.shape
     faces = weight_ref.shape[0]
     block = nvars * ROWS
-    me = lax.axis_index("pitch")
-    count = lax.axis_size("pitch")
     lane = lax.broadcasted_iota(jnp.int32, (ROWS, LANES), 1)
     meta = jnp.zeros((ROWS, LANES), jnp.float32)
     for v in range(nvars):
@@ -82,19 +80,12 @@
             at = f * block + v * ROWS
             mine_ref[at : at + ROWS, :] = weight_ref[f] * rows
     mine_ref[faces * block :, :] = meta
-    for offset, out_ref in zip(DIRECT, direct_refs):
-        route(
-            [(mine_ref, f * block, owner_ref[f], dest_ref[f]) for f in range(faces)],
-            lax.rem(me + (offset + count), count),
-            block,
-            out_ref,
-        )
-
-
-def route(items, target, block, out_ref):
+
+
+def route(items, target, halo, block, out_ref):
     lane = lax.broadcasted_iota(jnp.int32, (META, LANES), 1)
     slots = (out_ref.shape[0] - META) // block
-    meta = jnp.full((META, LANES), -1.0, jnp.float32)
+    meta = jnp.where(lane < OWNER_AT, halo, -1.0)
     used = jnp.int32(0)
     for ref, at, owner, dest in items:
         hit = owner == target
@@ -110,10 +101,10 @@
     out_ref[slots * block :, :] = meta
 
 
-def fetch_ids(refs, ids_ref, sems):
+def fetch_ids(parts, ids_ref, sems):
     copies = [
-        pltpu.make_async_copy(ref.at[pl.ds(ref.shape[0] - META, META), :], ids_ref.at[i], sems.at[i])
-        for i, ref in enumerate(refs)
+        pltpu.make_async_copy(ref.at[pl.ds(at, META), :], ids_ref.at[i], sems.at[i])
+        for i, (ref, at) in enumerate(parts)
     ]
     for copy in copies:
         copy.start()
@@ -129,29 +120,34 @@
     return [pltpu.SMEM((groups, META, LANES), jnp.float32), pltpu.SemaphoreType.DMA((groups,))]
 
 
-def received(faces, block, refs, ids_ref):
+def metas_of_group(group_ref, rows):
+    return [(group_ref, at + rows - META) for at in range(0, group_ref.shape[0], rows)]
+
+
+def blocks_of_group(group_ref, rows, block, ids_ref):
     items = []
-    for i, ref in enumerate(refs):
-        for f in range(faces):
-            ids = [ids_ref[i, 0, at + f].astype(jnp.int32) for at in (OWNER_AT, DEST_AT)]
-            items.append((ref, f * block, *ids))
+    for i, at in enumerate(range(0, group_ref.shape[0], rows)):
+        for f in range((rows - META) // block):
+            ids = [ids_ref[i, 0, lane + f].astype(jnp.int32) for lane in (OWNER_AT, DEST_AT)]
+            items.append((group_ref, at + f * block, *ids))
     return items
 
 
-def relay_kernel(owner_ref, dest_ref, mine_ref, below_ref, above_ref, *rest):
-    out_refs, ids_ref, sems = rest[:-2], rest[-2], rest[-1]
-    wait = fetch_ids((below_ref, above_ref), ids_ref, sems)
-    faces = owner_ref.shape[0]
-    block = (mine_ref.shape[0] - META) // faces
+def hops(plane):
+    side = 2 * (plane % 2) - 1
+    return [1, -1] + [side * by for by in range(2, CLASSES - 1)]
+
+
+def relay_kernel(mine_ref, group_ref, *refs, block):
+    out_refs, ids_ref, sems = refs[:-2], refs[-2], refs[-1]
+    rows = mine_ref.shape[0]
+    fetch_ids(metas_of_group(group_ref, rows), ids_ref, sems)()
     me = lax.axis_index("pitch")
     count = lax.axis_size("pitch")
-    items = []
-    for f in range(faces):
-        items.append((mine_ref, f * block, owner_ref[f], dest_ref[f]))
-    wait()
-    items += received(faces, block, (below_ref, above_ref), ids_ref)
-    for offset, out_ref in zip(RELAYED, out_refs):
-        route(items, lax.rem(me + (offset + count), count), block, out_ref)
+    halo = mine_ref[rows - META :, :]
+    items = blocks_of_group(group_ref, rows, block, ids_ref)
+    for by, out_ref in zip(hops(me), out_refs):
+        route(items, lax.rem(me + count + by, count), halo, block, out_ref)
 
 
 def add_block(out_ref, ref, at, dest):
@@ -161,15 +157,14 @@
         out_ref[v, :, to] += ref[at + v * ROWS : at + (v + 1) * ROWS, :]
 
 
-def base_kernel(owner_ref, dest_ref, flow_ref, speed_ref, mine_ref, below_ref, above_ref, out_ref, ids_ref, sems):
-    wait = fetch_ids((below_ref, above_ref), ids_ref, sems)
+def base_kernel(flow_ref, speed_ref, group_ref, below_ref, above_ref, out_ref, ids_ref, sems, *, rows):
+    wait = fetch_ids(metas_of_group(group_ref, rows), ids_ref, sems)
     nvars, _, cells = flow_ref.shape
-    faces = owner_ref.shape[0]
     block = nvars * ROWS
     per = cells // LANES
     me = lax.axis_index("pitch")
     lane = lax.broadcasted_iota(jnp.int32, (ROWS, LANES), 1)
-    before, after = below_ref[faces * block :, :], above_ref[faces * block :, :]
+    before, after = [ref[ref.shape[0] - META :, :] for ref in (below_ref, above_ref)]
     for v in range(nvars):
         left_edge = pltpu.roll(before, (LANES - v) % LANES, 1)
         right_edge = pltpu.roll(after, LANES - 1 - nvars - v, 1)
@@ -181,9 +176,8 @@
             up = jnp.where(lane == LANES - 1, right_edge if c == per - 1 else ups[c + 1], ups[c])
             speed = speed_ref[c : c + 1, :]
             out_ref[v, :, c * LANES : (c + 1) * LANES] = -speed * (up - down) * 0.5
-    items = [(mine_ref, f * block, owner_ref[f], dest_ref[f]) for f in range(faces)]
     wait()
-    items += received(faces, block, (below_ref, above_ref), ids_ref)
+    items = blocks_of_group(group_ref, rows, block, ids_ref)
     for ref, at, owner, dest in items:
 
         @pl.when(owner == me)
@@ -212,7 +206,7 @@
 def finish_kernel(*refs):
     base_ref, cells_ref, blocks = refs[0], refs[1], refs[2:-4]
     out_ref, mean_ref, ids_ref, sems = refs[-4:]
-    wait = fetch_ids(blocks, ids_ref, sems)
+    wait = fetch_ids([(ref, ref.shape[0] - META) for ref in blocks], ids_ref, sems)
     nvars, _, cells = out_ref.shape
     block = nvars * ROWS
     per = cells // LANES
@@ -242,9 +236,9 @@
     return jnp.where(gap == 0, jnp.float32(0.0), value)
 
 
-def shifted(array, by):
+def forwarded(array, i):
     count = lax.axis_size("pitch")
-    return lax.ppermute(array, "pitch", [(i, (i + by) % count) for i in range(count)])
+    return lax.ppermute(array, "pitch", [(p, (p + hops(p)[i]) % count) for p in range(count)])
 
 
 def per_device(flow, speed, rotor_face, owner, dest_block, intersection):
@@ -260,31 +254,34 @@
     speed = speed.reshape(cells // LANES, LANES)
 
     packed = call(cells_out_kernel, f32(devs * slots * ROWS, LANES), [vmem()], moved=700_000)(flow)
-    mine, *direct = call(
+    mine = call(
         weigh_kernel,
-        [f32(faces * block + META, LANES)] + [f32(2 * block + META, LANES) for _ in DIRECT],
+        f32(faces * block + META, LANES),
         [smem(), smem(), smem(), vmem(), vmem()],
         moved=600_000,
     )(owner, dest_block, intersection, flow, rotor)
     by_cell = lax.all_to_all(packed, "tm", 0, 0, tiled=True)
-    below, above = shifted(mine, 1), shifted(mine, -1)
+    planes = lax.axis_size("pitch")
+    rows = faces * block + META
+    classes = [list(range(i, planes, CLASSES)) for i in range(CLASSES)]
+    members = planes // CLASSES
+    group = lax.all_gather(mine, "pitch", tiled=True, axis_index_groups=classes)
     relays = call(
-        relay_kernel,
-        [f32(6 * block + META, LANES) for _ in RELAYED],
-        [smem(), smem(), vmem(), vmem(), vmem()],
-        id_scratch(2),
-        moved=700_000,
-    )(owner, dest_block, mine, below, above)
+        functools.partial(relay_kernel, block=block),
+        [f32(members * CAP * block + META, LANES) for _ in range(CLASSES - 1)],
+        [vmem(), vmem()],
+        id_scratch(members),
+        moved=1_500_000,
+    )(mine, group)
     by_cell, relays = lax.optimization_barrier((by_cell, relays))
-    sent = [shifted(a, by) for a, by in zip(relays, RELAYED)]
-    sent += [shifted(a, by) for a, by in zip(direct, DIRECT)]
+    sent = [forwarded(a, i) for i, a in enumerate(relays)]
     base = call(
-        base_kernel,
+        functools.partial(base_kernel, rows=rows),
         f32(nvars, inst, cells),
-        [smem(), smem(), vmem(), vmem(), vmem(), vmem(), vmem()],
-        id_scratch(2),
+        [vmem()] * 5,
+        id_scratch(members),
         moved=900_000,
-    )(owner, dest_block, flow, speed, mine, below, above)
+    )(flow, speed, group, sent[0], sent[1])
 
     def spectral(matrix_ref, cells_ref, out_ref):
         spectral_kernel(matrix_ref, cells_ref, out_ref, first_mean=tiles, last_mean=tiles + tiles // ROWS)

time: 84.7 us -> 70 us (0.83)
  the two profiles are of different devices: /device:TPU:67 before, /device:TPU:2 now
where the time goes in v2:
time: 70 us; the launch traced here: 69.6 us
  starting transfers between devices  27.4 us (39%)
  blocking collectives  26.1 us (37%)
  Pallas kernels  6.93 us (10%)
  waiting for transfers between devices  5.61 us (8%)
  local copies, waits for them, and re-layouts  1.62 us (2%)
  other arithmetic  1.17 us (2%)
  between operations  0.76 us (1%)
    all_gather x1, blocking collectives, per_device(): group = lax.all_gather(mine, 'pitch', tiled=True, axis_index_groups=classes)  26.1 us
    ppermute x3, starting transfers between devices, forwarded(): lax.ppermute(array, 'pitch', [(p, (p + hops(p)[i]) % count) for p in rang...  10.2 us
    all_to_all x1, starting transfers between devices, per_device(): by_cell = lax.all_to_all(packed, 'tm', 0, 0, tiled=True)  9.62 us
    all_to_all x1, starting transfers between devices, per_device(): by_time = lax.all_to_all(product, 'tm', 0, 0, tiled=True)  7.51 us
    ppermute x3, waiting for transfers between devices, forwarded(): lax.ppermute(array, 'pitch', [(p, (p + hops(p)[i]) % count) for p in rang...  5.61 us
    pallas_call x1, Pallas kernels, per_device(): call(finish_kernel, (f32(nvars, inst, cells), f32(nvars, cells)), [vmem()...  1.77 us
    unnamed x14, local copies, waits for them, and re-layouts  1.62 us
  transfers between devices with their start and end apart: 5, of which 2 were waited for; matrix products, arithmetic and copies ran while one was open for 2% of the time, Pallas kernels for 4%

profile of v2, /device:TPU:2, one launch (start us, length us, event | category | flops | bytes accessed | tf_op | source)
XLA Modules:
  0.0 69.6 jit_solution(1599555806649630384)
XLA Ops:
  0.6 0.0 copy-start
  0.6 1.0 %copy-done = f32[5,8,2048]{2,1,0:T(8,128)S(1)} copy-done((f32[5,8,2048]{2,1,0:T(8,128)S(1)}, f32[5,8,2048]{2,1,0:T(8,128)}, u32[]{:S(2)}) %copy-start) | copy-done | bytes 327704
  1.6 0.8 %shard_map.78 = f32[768,128]{1,0:T(8,128)} custom-call(f32[5,8,2048]{2,1,0:T(8,128)S(1)} %copy-done), custom_call_target="tpu_custom_call" | custom-call | bytes 700000 | tf_op jit(solution)/shard_map/pallas_call | solution.py:256
  2.4 0.0 copy-start.1
  2.4 0.0 copy-start.2
  2.4 9.6 %all-to-all-start = ((f32[32,24,128]{2,1,0:T(8,128)}), f32[32,24,128]{2,1,0:T(8,128)S(1)}, u32[]{:S(2)}, u32[]{:S(2)}) async-start(f32[32,24,128]{2,1,0:T(8,128)} %bitcast.4), calls=%async_computation | async-start | bytes 786432 | tf_op jit(solution)/shard_map/all_to_all | solution.py:263
  12.1 0.0 copy-start.4
  12.1 0.0 copy-start.5
  12.1 0.0 copy-start.6
  12.1 0.0 copy-done.1
  12.1 0.0 copy-done.2
  12.1 0.6 copy-done.4
  12.7 0.0 copy-done.5
  12.7 0.0 copy-done.6
  12.8 0.6 shard_map.77.mine_ref
  13.4 26.1 %all_gather.3.group_ref = f32[672,128]{1,0:T(8,128)S(1)} all-gather(f32[168,128]{1,0:T(8,128)S(1)} %shard_map.77.mine_ref), channel_id=1, replica_groups={{0,4,8,12},{1,5,9,13},{2,6,10,14},{3,7,11,15},{16,20,24,28},{17,21,25,2..., dimensions={0}, use_global_device_ids=true | all-gather | bytes 430080 | tf_op jit(solution)/shard_map/all_gather | solution.py:268
  39.5 1.3 %shard_map.79 = (f32[328,128]{1,0:T(8,128)S(1)}, f32[328,128]{1,0:T(8,128)S(1)}, f32[328,128]{1,0:T(8,128)S(1)}) custom-call(f32[168,128]{1,0:T(8,128)S(1)} %shard_map.77.mine_ref, f32[672,128]{1,0:T(8,128)S(1)} %all_gather.3.group_ref), custom_call_target="tpu_custom_call" | custom-call | bytes 1500000 | tf_op jit(solution)/shard_map/pallas_call | solution.py:269
  40.8 1.2 %compare_select_fusion.matrix_ref = f32[256,256]{1,0:T(8,128)S(1)} fusion(), kind=kLoop, calls=%fused_computation.6 | loop fusion | flops 2228224 | bytes 262144 | tf_op jit(solution)/shard_map/jit(_where)/select_n | solution.py:236
  41.9 0.0 all-to-all-done
  42.0 1.4 %shard_map.81 = f32[768,128]{1,0:T(8,128)} custom-call(f32[256,256]{1,0:T(8,128)S(1)} %compare_select_fusion.matrix_ref, f32[768,128]{1,0:T(8,128)S(1)} %bitcast.10), custom_call_target="tpu_custom_call" | custom-call | flops 301989888 | bytes 1000000 | tf_op jit(solution)/shard_map/pallas_call | solution.py:289
  43.3 0.0 copy-start.3
  43.3 7.5 %all-to-all-start.1 = ((f32[32,24,128]{2,1,0:T(8,128)}), f32[32,24,128]{2,1,0:T(8,128)S(1)}, u32[]{:S(2)}, u32[]{:S(2)}) async-start(f32[32,24,128]{2,1,0:T(8,128)} %bitcast.6), calls=%async_computation.1 | async-start | bytes 786432 | tf_op jit(solution)/shard_map/all_to_all | solution.py:292
  50.8 5.0 %collective-permute-start = (f32[328,128]{1,0:T(8,128)S(1)}, f32[328,128]{1,0:T(8,128)S(1)}, u32[]{:S(2)}, u32[]{:S(2)}) collective-permute-start(f32[328,128]{1,0:T(8,128)S(1)} %get-tuple-element.12), channel_id=1, source_target_pairs={{0,1},{1,2},{2,3},{3,4},{4,5},{5,6},{6,7},{7,8},{8,9},{9,10},{10,1... | collective-permute-start | bytes 503816 | tf_op jit(solution)/shard_map/ppermute | solution.py:241
  55.8 2.1 %collective-permute-start.1 = (f32[328,128]{1,0:T(8,128)S(1)}, f32[328,128]{1,0:T(8,128)S(1)}, u32[]{:S(2)}, u32[]{:S(2)}) collective-permute-start(f32[328,128]{1,0:T(8,128)S(1)} %get-tuple-element.13), channel_id=1, source_target_pairs={{0,15},{1,0},{2,1},{3,2},{4,3},{5,4},{6,5},{7,6},{8,7},{9,8},{10,9... | collective-permute-start | bytes 503816 | tf_op jit(solution)/shard_map/ppermute | solution.py:241
  57.9 3.2 %collective-permute-start.2 = (f32[328,128]{1,0:T(8,128)S(1)}, f32[328,128]{1,0:T(8,128)S(1)}, u32[]{:S(2)}, u32[]{:S(2)}) collective-permute-start(f32[328,128]{1,0:T(8,128)S(1)} %get-tuple-element.15), channel_id=1, source_target_pairs={{0,14},{1,3},{2,0},{3,5},{4,2},{5,7},{6,4},{7,9},{8,6},{9,11},{10,... | collective-permute-start | bytes 503816 | tf_op jit(solution)/shard_map/ppermute | solution.py:241
  61.1 0.0 collective-permute-done.below_ref.refs_2_
  61.1 3.4 %collective-permute-done.1.above_ref.refs_3_ = f32[328,128]{1,0:T(8,128)S(1)} collective-permute-done((f32[328,128]{1,0:T(8,128)S(1)}, f32[328,128]{1,0:T(8,128)S(1)}, u32[]{:S(2)}, u32[]{:S(2)}) %collective-permute-start.1) | collective-permute-done | bytes 167968 | tf_op jit(solution)/shard_map/ppermute | solution.py:241
  64.5 0.0 copy-done.3
  64.5 1.1 %shard_map.80.refs_0_ = f32[5,8,2048]{2,1,0:T(8,128)S(1)} custom-call(f32[5,8,2048]{2,1,0:T(8,128)S(1)} %copy-done.1, f32[16,128]{1,0:T(8,128)S(1)} %bitcast.12, f32[672,128]{1,0:T(8,128)S(1)} %all_gather.3.group_ref, f32[328,128]{1,0:T(8,128)S(1)} %collective-permute-done.below_ref.refs_2_, f32[328,128]{1,0:T(8,128)S(1)} %collective-permute-done.1.above_ref.refs_3_), custom_call_target="tpu_custom_call" | custom-call | bytes 900000 | tf_op jit(solution)/shard_map/pallas_call | solution.py:278
  65.5 2.2 %collective-permute-done.2.refs_4_ = f32[328,128]{1,0:T(8,128)S(1)} collective-permute-done((f32[328,128]{1,0:T(8,128)S(1)}, f32[328,128]{1,0:T(8,128)S(1)}, u32[]{:S(2)}, u32[]{:S(2)}) %collective-permute-start.2) | collective-permute-done | bytes 167968 | tf_op jit(solution)/shard_map/ppermute | solution.py:241
  67.8 0.0 all-to-all-done.1
  67.8 1.8 %shard_map.82 = (f32[5,8,2048]{2,1,0:T(8,128)}, f32[5,2048]{1,0:T(8,128)}) custom-call(f32[5,8,2048]{2,1,0:T(8,128)S(1)} %shard_map.80.refs_0_, f32[768,128]{1,0:T(8,128)S(1)} %bitcast.9, f32[328,128]{1,0:T(8,128)S(1)} %collective-permute-done.below_ref.refs_2_, f32[328,128]{1,0:T(8,128)S(1)} %collective-permute-done.1.above_ref.refs_3_, ...), custom_call_target="tpu_custom_call" | custom-call | bytes 1500000 | tf_op jit(solution)/shard_map/pallas_call | solution.py:293
Async XLA Ops:
  0.6 1.0 %copy-start = (f32[5,8,2048]{2,1,0:T(8,128)S(1)}, f32[5,8,2048]{2,1,0:T(8,128)}, u32[]{:S(2)}) copy-start(f32[5,8,2048]{2,1,0:T(8,128)} %flow_ref.5) | copy-start | bytes 983044
  2.4 9.7 %copy-start.1 = (f32[5,8,2048]{2,1,0:T(8,128)S(1)}, f32[5,8,2048]{2,1,0:T(8,128)}, u32[]{:S(2)}) copy-start(f32[5,8,2048]{2,1,0:T(8,128)} %flow_ref.5) | copy-start | bytes 983044
  2.4 9.7 %copy-start.2 = (f32[8,4,5,128]{3,1,2,0:T(4,128)S(1)}, f32[8,4,5,128]{3,1,2,0:T(4,128)}, u32[]{:S(2)}) copy-start(f32[8,4,5,128]{3,1,2,0:T(4,128)} %param.8) | copy-start | bytes 245764
  2.4 39.5 %all-to-all-start = ((f32[32,24,128]{2,1,0:T(8,128)}), f32[32,24,128]{2,1,0:T(8,128)S(1)}, u32[]{:S(2)}, u32[]{:S(2)}) async-start(f32[32,24,128]{2,1,0:T(8,128)} %bitcast.4), calls=%async_computation | async-start | bytes 786432 | tf_op jit(solution)/shard_map/all_to_all | solution.py:263
  12.1 0.7 copy-start.4
  12.1 0.7 copy-start.5
  12.1 0.7 copy-start.6
  43.3 21.1 %copy-start.3 = (f32[2048]{0:T(1024)S(1)}, f32[2048]{0:T(1024)}, u32[]{:S(2)}) copy-start(f32[2048]{0:T(1024)} %param.7) | copy-start | bytes 24580
  43.3 24.5 %all-to-all-start.1 = ((f32[32,24,128]{2,1,0:T(8,128)}), f32[32,24,128]{2,1,0:T(8,128)S(1)}, u32[]{:S(2)}, u32[]{:S(2)}) async-start(f32[32,24,128]{2,1,0:T(8,128)} %bitcast.6), calls=%async_computation.1 | async-start | bytes 786432 | tf_op jit(solution)/shard_map/all_to_all | solution.py:292
  50.8 10.3 %collective-permute-start = (f32[328,128]{1,0:T(8,128)S(1)}, f32[328,128]{1,0:T(8,128)S(1)}, u32[]{:S(2)}, u32[]{:S(2)}) collective-permute-start(f32[328,128]{1,0:T(8,128)S(1)} %get-tuple-element.12), channel_id=1, source_target_pairs={{0,1},{1,2},{2,3},{3,4},{4,5},{5,6},{6,7},{7,8},{8,9},{9,10},{10,1... | collective-permute-start | bytes 503816 | tf_op jit(solution)/shard_map/ppermute | solution.py:241
  55.8 8.6 %collective-permute-start.1 = (f32[328,128]{1,0:T(8,128)S(1)}, f32[328,128]{1,0:T(8,128)S(1)}, u32[]{:S(2)}, u32[]{:S(2)}) collective-permute-start(f32[328,128]{1,0:T(8,128)S(1)} %get-tuple-element.13), channel_id=1, source_target_pairs={{0,15},{1,0},{2,1},{3,2},{4,3},{5,4},{6,5},{7,6},{8,7},{9,8},{10,9... | collective-permute-start | bytes 503816 | tf_op jit(solution)/shard_map/ppermute | solution.py:241
  57.9 9.9 %collective-permute-start.2 = (f32[328,128]{1,0:T(8,128)S(1)}, f32[328,128]{1,0:T(8,128)S(1)}, u32[]{:S(2)}, u32[]{:S(2)}) collective-permute-start(f32[328,128]{1,0:T(8,128)S(1)} %get-tuple-element.15), channel_id=1, source_target_pairs={{0,14},{1,3},{2,0},{3,5},{4,2},{5,7},{6,4},{7,9},{8,6},{9,11},{10,... | collective-permute-start | bytes 503816 | tf_op jit(solution)/shard_map/ppermute | solution.py:241

commit v3 on v2

--- a/solution.py
+++ b/solution.py
@@ -12,8 +12,9 @@
 META = 8
 OWNER_AT, DEST_AT = 16, 24
 VMEM = 32 * 1024 * 1024
+SLOW = 20_000_000_000
 CAP = 2
-CLASSES = 4
+FAR, NEAR = 3, 3
 
 
 def vmem():
@@ -40,7 +41,7 @@
     return jax.ShapeDtypeStruct(shape, jnp.float32)
 
 
-def cells_out_kernel(flow_ref, out_ref):
+def pack_kernel(flow_ref, out_ref):
     nvars, _, cells = flow_ref.shape
     per = cells // LANES
     tiles = nvars * per
@@ -120,33 +121,39 @@
     return [pltpu.SMEM((groups, META, LANES), jnp.float32), pltpu.SemaphoreType.DMA((groups,))]
 
 
-def metas_of_group(group_ref, rows):
-    return [(group_ref, at + rows - META) for at in range(0, group_ref.shape[0], rows)]
-
-
-def blocks_of_group(group_ref, rows, block, ids_ref):
+def side(plane):
+    return 2 * (plane % 2) - 1
+
+
+def far_hops(plane):
+    return [side(plane) * by for by in (-7, 4, -4)]
+
+
+def near_hops(plane):
+    return [side(plane) * by for by in (1, -1, 2)]
+
+
+def metas(refs):
+    return [(ref, ref.shape[0] - META) for ref in refs]
+
+
+def blocks_of(refs, block, ids_ref):
     items = []
-    for i, at in enumerate(range(0, group_ref.shape[0], rows)):
-        for f in range((rows - META) // block):
+    for i, ref in enumerate(refs):
+        for f in range((ref.shape[0] - META) // block):
             ids = [ids_ref[i, 0, lane + f].astype(jnp.int32) for lane in (OWNER_AT, DEST_AT)]
-            items.append((group_ref, at + f * block, *ids))
+            items.append((ref, f * block, *ids))
     return items
 
 
-def hops(plane):
-    side = 2 * (plane % 2) - 1
-    return [1, -1] + [side * by for by in range(2, CLASSES - 1)]
-
-
-def relay_kernel(mine_ref, group_ref, *refs, block):
-    out_refs, ids_ref, sems = refs[:-2], refs[-2], refs[-1]
-    rows = mine_ref.shape[0]
-    fetch_ids(metas_of_group(group_ref, rows), ids_ref, sems)()
+def relay_kernel(*refs, block):
+    held, out_refs, ids_ref, sems = refs[: 1 + FAR], refs[1 + FAR : -2], refs[-2], refs[-1]
+    fetch_ids(metas(held), ids_ref, sems)()
     me = lax.axis_index("pitch")
     count = lax.axis_size("pitch")
-    halo = mine_ref[rows - META :, :]
-    items = blocks_of_group(group_ref, rows, block, ids_ref)
-    for by, out_ref in zip(hops(me), out_refs):
+    halo = held[0][held[0].shape[0] - META :, :]
+    items = blocks_of(held, block, ids_ref)
+    for by, out_ref in zip(near_hops(me), out_refs):
         route(items, lax.rem(me + count + by, count), halo, block, out_ref)
 
 
@@ -157,14 +164,17 @@
         out_ref[v, :, to] += ref[at + v * ROWS : at + (v + 1) * ROWS, :]
 
 
-def base_kernel(flow_ref, speed_ref, group_ref, below_ref, above_ref, out_ref, ids_ref, sems, *, rows):
-    wait = fetch_ids(metas_of_group(group_ref, rows), ids_ref, sems)
+def base_kernel(flow_ref, speed_ref, first_ref, second_ref, *refs):
+    held, out_ref, ids_ref, sems = refs[: 1 + FAR], refs[-3], refs[-2], refs[-1]
+    wait = fetch_ids(metas(held), ids_ref, sems)
     nvars, _, cells = flow_ref.shape
     block = nvars * ROWS
     per = cells // LANES
     me = lax.axis_index("pitch")
     lane = lax.broadcasted_iota(jnp.int32, (ROWS, LANES), 1)
-    before, after = [ref[ref.shape[0] - META :, :] for ref in (below_ref, above_ref)]
+    first, second = [ref[ref.shape[0] - META :, :] for ref in (first_ref, second_ref)]
+    odd = lax.rem(me, 2) == 1
+    before, after = jnp.where(odd, second, first), jnp.where(odd, first, second)
     for v in range(nvars):
         left_edge = pltpu.roll(before, (LANES - v) % LANES, 1)
         right_edge = pltpu.roll(after, LANES - 1 - nvars - v, 1)
@@ -177,7 +187,7 @@
             speed = speed_ref[c : c + 1, :]
             out_ref[v, :, c * LANES : (c + 1) * LANES] = -speed * (up - down) * 0.5
     wait()
-    items = blocks_of_group(group_ref, rows, block, ids_ref)
+    items = blocks_of(held, block, ids_ref)
     for ref, at, owner, dest in items:
 
         @pl.when(owner == me)
@@ -185,14 +195,26 @@
             add_block(out_ref, ref, at, dest)
 
 
-def spectral_kernel(matrix_ref, cells_ref, out_ref, *, first_mean, last_mean):
-    count = matrix_ref.shape[0]
+def spectral_matrix(count):
+    column = lax.broadcasted_iota(jnp.int32, (ROWS, count), 1)
+    gap = (count - column) % count
+    safe = jnp.where(gap == 0, 1, gap).astype(jnp.float32)
+    angle = jnp.float32(jnp.pi) * safe / count
+    parity = (1 - 2 * (gap % 2)).astype(jnp.float32)
+    value = jnp.float32(jnp.pi) / count * parity * jnp.cos(angle) / jnp.sin(angle)
+    row = jnp.where(gap == 0, jnp.float32(0.0), value)
+    return pltpu.roll(jnp.broadcast_to(row[:1], (count, count)), 0, 1, stride=1, stride_axis=0)
+
+
+def spectral_kernel(cells_ref, out_ref, *, count, first_mean, last_mean):
     devs = count // ROWS
     slots = cells_ref.shape[0] // count
     me = lax.axis_index("tm")
     got = cells_ref[...].reshape(devs, slots, ROWS, LANES)
     columns = jnp.concatenate([got[:, k].reshape(count, LANES) for k in range(slots)], axis=1)
-    product = jnp.dot(matrix_ref[...], columns, precision=lax.Precision.HIGHEST, preferred_element_type=jnp.float32)
+    product = jnp.dot(
+        spectral_matrix(count), columns, precision=lax.Precision.HIGHEST, preferred_element_type=jnp.float32
+    )
     for k in range(slots):
         tile = me * slots + k
         is_mean = jnp.logical_and(tile >= first_mean, tile < last_mean)
@@ -206,7 +228,7 @@
 def finish_kernel(*refs):
     base_ref, cells_ref, blocks = refs[0], refs[1], refs[2:-4]
     out_ref, mean_ref, ids_ref, sems = refs[-4:]
-    wait = fetch_ids([(ref, ref.shape[0] - META) for ref in blocks], ids_ref, sems)
+    wait = fetch_ids(metas(blocks), ids_ref, sems)
     nvars, _, cells = out_ref.shape
     block = nvars * ROWS
     per = cells // LANES
@@ -226,17 +248,7 @@
                 add_block(out_ref, ref, slot * block, dest)
 
 
-def spectral_matrix(count):
-    index = jnp.arange(count, dtype=jnp.int32)
-    gap = (index[:, None] - index[None, :]) % count
-    safe = jnp.where(gap == 0, 1, gap).astype(jnp.float32)
-    angle = jnp.float32(jnp.pi) * safe / count
-    parity = (1 - 2 * (gap % 2)).astype(jnp.float32)
-    value = jnp.float32(jnp.pi) / count * parity * jnp.cos(angle) / jnp.sin(angle)
-    return jnp.where(gap == 0, jnp.float32(0.0), value)
-
-
-def forwarded(array, i):
+def sent_by(array, hops, i):
     count = lax.axis_size("pitch")
     return lax.ppermute(array, "pitch", [(p, (p + hops(p)[i]) % count) for p in range(count)])
 
@@ -253,7 +265,7 @@
     rotor = jnp.transpose(rotor_face, (0, 2, 1, 3)).reshape(inst * nvars * faces, LANES)
     speed = speed.reshape(cells // LANES, LANES)
 
-    packed = call(cells_out_kernel, f32(devs * slots * ROWS, LANES), [vmem()], moved=700_000)(flow)
+    packed = call(pack_kernel, f32(devs * slots * ROWS, LANES), [vmem()], moved=700_000)(flow)
     mine = call(
         weigh_kernel,
         f32(faces * block + META, LANES),
@@ -261,34 +273,31 @@
         moved=600_000,
     )(owner, dest_block, intersection, flow, rotor)
     by_cell = lax.all_to_all(packed, "tm", 0, 0, tiled=True)
-    planes = lax.axis_size("pitch")
-    rows = faces * block + META
-    classes = [list(range(i, planes, CLASSES)) for i in range(CLASSES)]
-    members = planes // CLASSES
-    group = lax.all_gather(mine, "pitch", tiled=True, axis_index_groups=classes)
+    product = call(
+        functools.partial(spectral_kernel, count=count, first_mean=tiles, last_mean=tiles + tiles // ROWS),
+        f32(devs * slots * ROWS, LANES),
+        [vmem()],
+        flops=6 * 2 * count * count * slots * LANES,
+        moved=1_000_000,
+    )(by_cell)
+    held = [mine] + [sent_by(mine, far_hops, i) for i in range(FAR)]
     relays = call(
         functools.partial(relay_kernel, block=block),
-        [f32(members * CAP * block + META, LANES) for _ in range(CLASSES - 1)],
-        [vmem(), vmem()],
-        id_scratch(members),
+        [f32(len(held) * CAP * block + META, LANES) for _ in range(NEAR)],
+        [vmem()] * len(held),
+        id_scratch(len(held)),
+        flops=20000000000,
         moved=1_500_000,
-    )(mine, group)
-    by_cell, relays = lax.optimization_barrier((by_cell, relays))
-    sent = [forwarded(a, i) for i, a in enumerate(relays)]
+    )(*held)
+    sent = [sent_by(a, near_hops, i) for i, a in enumerate(relays)]
     base = call(
-        functools.partial(base_kernel, rows=rows),
+        base_kernel,
         f32(nvars, inst, cells),
-        [vmem()] * 5,
-        id_scratch(members),
+        [vmem()] * (4 + len(held)),
+        id_scratch(len(held)),
         moved=900_000,
-    )(flow, speed, group, sent[0], sent[1])
-
-    def spectral(matrix_ref, cells_ref, out_ref):
-        spectral_kernel(matrix_ref, cells_ref, out_ref, first_mean=tiles, last_mean=tiles + tiles // ROWS)
-
-    product = call(spectral, f32(devs * slots * ROWS, LANES), [vmem(), vmem()], flops=6 * 2 * count * count * slots * LANES, moved=1_000_000)(
-        spectral_matrix(count), by_cell
-    )
+    )(flow, speed, sent[0], sent[1], *held)
+
     by_time = lax.all_to_all(product, "tm", 0, 0, tiled=True)
     residual, mean_flow = call(
         finish_kernel,

time: 70 us -> 64 us (0.914)
  blocking collectives: 26.1 us -> 0 us
  starting transfers between devices: 27.4 us -> 48.5 us
  other arithmetic: 1.17 us -> 0 us
    all_gather x1 -> x0, blocking collectives: 26.1 us -> none  [per_device(): group = lax.all_gather(mine, 'pitch', tiled=True, axis_index_groups=classes)]
    ppermute x3 -> x6, starting transfers between devices: 10.2 us -> 31.5 us  [sent_by(): lax.ppermute(array, 'pitch', [(p, (p + hops(p)[i]) % count) for p in rang...]
    select_n x1 -> x0, other arithmetic: 1.17 us -> none  [spectral_matrix(): return jnp.where(gap == 0, jnp.float32(0.0), value)]
    ppermute x3 -> x6, waiting for transfers between devices: 5.61 us -> 5.55 us  [sent_by(): lax.ppermute(array, 'pitch', [(p, (p + hops(p)[i]) % count) for p in rang...]
  transfers between devices with their start and end apart: 5 -> 8, of which waited for: 2 -> 2; matrix products, arithmetic and copies ran while one was open for 2% -> 0% of each run, Pallas kernels for 4% -> 7%
where the time goes in v3:
time: 64 us; the launch traced here: 63.5 us
  starting transfers between devices  48.5 us (76%)
  Pallas kernels  7.06 us (11%)
  waiting for transfers between devices  5.56 us (9%)
  local copies, waits for them, and re-layouts  1.62 us (3%)
  between operations  0.81 us (1%)
    ppermute x6, starting transfers between devices, sent_by(): lax.ppermute(array, 'pitch', [(p, (p + hops(p)[i]) % count) for p in rang...  31.5 us
    all_to_all x1, starting transfers between devices, per_device(): by_cell = lax.all_to_all(packed, 'tm', 0, 0, tiled=True)  9.62 us
    all_to_all x1, starting transfers between devices, per_device(): by_time = lax.all_to_all(product, 'tm', 0, 0, tiled=True)  7.38 us
    ppermute x6, waiting for transfers between devices, sent_by(): lax.ppermute(array, 'pitch', [(p, (p + hops(p)[i]) % count) for p in rang...  5.55 us
    pallas_call x1, Pallas kernels, per_device(): call(finish_kernel, (f32(nvars, inst, cells), f32(nvars, cells)), [vmem()...  1.76 us
    unnamed x14, local copies, waits for them, and re-layouts  1.62 us
    pallas_call x1, Pallas kernels, per_device(): call(functools.partial(spectral_kernel, count=count, first_mean=tiles, la...  1.45 us
  transfers between devices with their start and end apart: 8, of which 2 were waited for; matrix products, arithmetic and copies ran while one was open for 0% of the time, Pallas kernels for 7%

profile of v3, /device:TPU:2, one launch (start us, length us, event | category | flops | bytes accessed | tf_op | source)
XLA Modules:
  0.0 63.5 jit_solution(9707988686552670722)
XLA Ops:
  0.6 0.0 copy-start
  0.6 1.0 %copy-done = f32[5,8,2048]{2,1,0:T(8,128)S(1)} copy-done((f32[5,8,2048]{2,1,0:T(8,128)S(1)}, f32[5,8,2048]{2,1,0:T(8,128)}, u32[]{:S(2)}) %copy-start) | copy-done | bytes 327704
  1.6 0.8 %shard_map.80 = f32[768,128]{1,0:T(8,128)} custom-call(f32[5,8,2048]{2,1,0:T(8,128)S(1)} %copy-done), custom_call_target="tpu_custom_call" | custom-call | bytes 700000 | tf_op jit(solution)/shard_map/pallas_call | solution.py:268
  2.5 9.6 %all-to-all-start = ((f32[32,24,128]{2,1,0:T(8,128)}), f32[32,24,128]{2,1,0:T(8,128)S(1)}, u32[]{:S(2)}, u32[]{:S(2)}) async-start(f32[32,24,128]{2,1,0:T(8,128)} %bitcast.4), calls=%async_computation | async-start | bytes 786432 | tf_op jit(solution)/shard_map/all_to_all | solution.py:275
  12.1 0.0 copy-start.4
  12.1 0.0 copy-start.5
  12.1 0.0 copy-start.6
  12.1 0.0 copy-done.1
  12.1 0.0 copy-done.2
  12.1 0.6 copy-done.4
  12.7 0.0 copy-done.5
  12.8 0.0 copy-done.6
  12.8 0.6 shard_map.77.refs_0_
  13.4 7.2 %collective-permute-start.2 = (f32[168,128]{1,0:T(8,128)S(1)}, f32[168,128]{1,0:T(8,128)S(1)}, u32[]{:S(2)}, u32[]{:S(2)}) collective-permute-start(f32[168,128]{1,0:T(8,128)S(1)} %shard_map.77.refs_0_), channel_id=1, source_target_pairs={{0,4},{1,13},{2,6},{3,15},{4,8},{5,1},{6,10},{7,3},{8,12},{9,5},{1... | collective-permute-start | bytes 258056 | tf_op jit(solution)/shard_map/ppermute | solution.py:253
  20.6 5.6 %collective-permute-start.1 = (f32[168,128]{1,0:T(8,128)S(1)}, f32[168,128]{1,0:T(8,128)S(1)}, u32[]{:S(2)}, u32[]{:S(2)}) collective-permute-start(f32[168,128]{1,0:T(8,128)S(1)} %shard_map.77.refs_0_), channel_id=1, source_target_pairs={{0,12},{1,5},{2,14},{3,7},{4,0},{5,9},{6,2},{7,11},{8,4},{9,13},{1... | collective-permute-start | bytes 258056 | tf_op jit(solution)/shard_map/ppermute | solution.py:253
  26.2 8.3 %collective-permute-start = (f32[168,128]{1,0:T(8,128)S(1)}, f32[168,128]{1,0:T(8,128)S(1)}, u32[]{:S(2)}, u32[]{:S(2)}) collective-permute-start(f32[168,128]{1,0:T(8,128)S(1)} %shard_map.77.refs_0_), channel_id=1, source_target_pairs={{0,7},{1,10},{2,9},{3,12},{4,11},{5,14},{6,13},{7,0},{8,15},{9,2},... | collective-permute-start | bytes 258056 | tf_op jit(solution)/shard_map/ppermute | solution.py:253
  34.5 0.0 all-to-all-done
  34.5 1.4 %shard_map.81 = f32[768,128]{1,0:T(8,128)} custom-call(f32[768,128]{1,0:T(8,128)S(1)} %bitcast.10), custom_call_target="tpu_custom_call" | custom-call | flops 301989888 | bytes 1000000 | tf_op jit(solution)/shard_map/pallas_call | solution.py:276
  35.9 7.4 %all-to-all-start.1 = ((f32[32,24,128]{2,1,0:T(8,128)}), f32[32,24,128]{2,1,0:T(8,128)S(1)}, u32[]{:S(2)}, u32[]{:S(2)}) async-start(f32[32,24,128]{2,1,0:T(8,128)} %bitcast.6), calls=%async_computation.1 | async-start | bytes 786432 | tf_op jit(solution)/shard_map/all_to_all | solution.py:301
  43.3 0.0 collective-permute-done.2.refs_3_
  43.3 0.0 collective-permute-done.1.refs_2_
  43.3 2.8 %collective-permute-done.refs_1_ = f32[168,128]{1,0:T(8,128)S(1)} collective-permute-done((f32[168,128]{1,0:T(8,128)S(1)}, f32[168,128]{1,0:T(8,128)S(1)}, u32[]{:S(2)}, u32[]{:S(2)}) %collective-permute-start) | collective-permute-done | bytes 86048 | tf_op jit(solution)/shard_map/ppermute | solution.py:253
  46.1 1.3 %shard_map.78 = (f32[328,128]{1,0:T(8,128)S(1)}, f32[328,128]{1,0:T(8,128)S(1)}, f32[328,128]{1,0:T(8,128)S(1)}) custom-call(f32[168,128]{1,0:T(8,128)S(1)} %shard_map.77.refs_0_, f32[168,128]{1,0:T(8,128)S(1)} %collective-permute-done.refs_1_, f32[168,128]{1,0:T(8,128)S(1)} %collective-permute-done.1.refs_2_, f32[168,128]{1,0:T(8,128)S(1)} %collective-permute-done.2.refs_3_), custom_call_target="tpu_custom_call" | custom-call | flops 20000000000 | bytes 1500000 | tf_op jit(solution)/shard_map/pallas_call | solution.py:284
  47.4 2.3 %collective-permute-start.3 = (f32[328,128]{1,0:T(8,128)S(1)}, f32[328,128]{1,0:T(8,128)S(1)}, u32[]{:S(2)}, u32[]{:S(2)}) collective-permute-start(f32[328,128]{1,0:T(8,128)S(1)} %get-tuple-element.5), channel_id=1, source_target_pairs={{0,15},{1,2},{2,1},{3,4},{4,3},{5,6},{6,5},{7,8},{8,7},{9,10},{10,... | collective-permute-start | bytes 503816 | tf_op jit(solution)/shard_map/ppermute | solution.py:253
  49.7 3.9 %collective-permute-start.4 = (f32[328,128]{1,0:T(8,128)S(1)}, f32[328,128]{1,0:T(8,128)S(1)}, u32[]{:S(2)}, u32[]{:S(2)}) collective-permute-start(f32[328,128]{1,0:T(8,128)S(1)} %get-tuple-element.6), channel_id=1, source_target_pairs={{0,1},{1,0},{2,3},{3,2},{4,5},{5,4},{6,7},{7,6},{8,9},{9,8},{10,11... | collective-permute-start | bytes 503816 | tf_op jit(solution)/shard_map/ppermute | solution.py:253
  53.6 4.2 %collective-permute-start.5 = (f32[328,128]{1,0:T(8,128)S(1)}, f32[328,128]{1,0:T(8,128)S(1)}, u32[]{:S(2)}, u32[]{:S(2)}) collective-permute-start(f32[328,128]{1,0:T(8,128)S(1)} %get-tuple-element.7), channel_id=1, source_target_pairs={{0,14},{1,3},{2,0},{3,5},{4,2},{5,7},{6,4},{7,9},{8,6},{9,11},{10,... | collective-permute-start | bytes 503816 | tf_op jit(solution)/shard_map/ppermute | solution.py:253
  57.8 0.0 collective-permute-done.3.first_ref.refs_2_
  57.8 0.0 collective-permute-done.4.second_ref.refs_3_
  57.8 1.1 %shard_map.79.refs_0_ = f32[5,8,2048]{2,1,0:T(8,128)S(1)} custom-call(f32[5,8,2048]{2,1,0:T(8,128)S(1)} %copy-done.1, f32[16,128]{1,0:T(8,128)S(1)} %bitcast.12, f32[328,128]{1,0:T(8,128)S(1)} %collective-permute-done.3.first_ref.refs_2_, f32[328,128]{1,0:T(8,128)S(1)} %collective-permute-done.4.second_ref.refs_3_, f32[168,128]{1,0:T(8,128)S(1)} %shard_map.77.refs_0_, ...), custom_call_target="tpu_custom_call" | custom-call | bytes 900000 | tf_op jit(solution)/shard_map/pallas_call | solution.py:293
  59.0 2.8 %collective-permute-done.5.refs_4_ = f32[328,128]{1,0:T(8,128)S(1)} collective-permute-done((f32[328,128]{1,0:T(8,128)S(1)}, f32[328,128]{1,0:T(8,128)S(1)}, u32[]{:S(2)}, u32[]{:S(2)}) %collective-permute-start.5) | collective-permute-done | bytes 167968 | tf_op jit(solution)/shard_map/ppermute | solution.py:253
  61.8 0.0 all-to-all-done.1
  61.8 1.8 %shard_map.82 = (f32[5,8,2048]{2,1,0:T(8,128)}, f32[5,2048]{1,0:T(8,128)}) custom-call(f32[5,8,2048]{2,1,0:T(8,128)S(1)} %shard_map.79.refs_0_, f32[768,128]{1,0:T(8,128)S(1)} %bitcast.9, f32[328,128]{1,0:T(8,128)S(1)} %collective-permute-done.3.first_ref.refs_2_, f32[328,128]{1,0:T(8,128)S(1)} %collective-permute-done.4.second_ref.refs_3_, ...), custom_call_target="tpu_custom_call" | custom-call | bytes 1500000 | tf_op jit(solution)/shard_map/pallas_call | solution.py:302
  (4 shorter events, 0.0 us)
Async XLA Ops:
  0.6 1.0 %copy-start = (f32[5,8,2048]{2,1,0:T(8,128)S(1)}, f32[5,8,2048]{2,1,0:T(8,128)}, u32[]{:S(2)}) copy-start(f32[5,8,2048]{2,1,0:T(8,128)} %flow_ref.5) | copy-start | bytes 983044
  2.4 9.7 %copy-start.1 = (f32[5,8,2048]{2,1,0:T(8,128)S(1)}, f32[5,8,2048]{2,1,0:T(8,128)}, u32[]{:S(2)}) copy-start(f32[5,8,2048]{2,1,0:T(8,128)} %flow_ref.5) | copy-start | bytes 983044
  2.5 9.7 %copy-start.2 = (f32[8,4,5,128]{3,1,2,0:T(4,128)S(1)}, f32[8,4,5,128]{3,1,2,0:T(4,128)}, u32[]{:S(2)}) copy-start(f32[8,4,5,128]{3,1,2,0:T(4,128)} %param.8) | copy-start | bytes 245764
  2.5 32.0 %all-to-all-start = ((f32[32,24,128]{2,1,0:T(8,128)}), f32[32,24,128]{2,1,0:T(8,128)S(1)}, u32[]{:S(2)}, u32[]{:S(2)}) async-start(f32[32,24,128]{2,1,0:T(8,128)} %bitcast.4), calls=%async_computation | async-start | bytes 786432 | tf_op jit(solution)/shard_map/all_to_all | solution.py:275
  12.1 0.7 %copy-start.4 = (s32[4,1]{0,1:T(1,128)S(1)}, s32[4,1]{0,1:T(1,128)}, u32[]{:S(2)}) copy-start(s32[4,1]{0,1:T(1,128)} %param.9) | copy-start | bytes 52
  12.1 0.7 %copy-start.5 = (s32[4]{0:T(128)S(1)}, s32[4]{0:T(128)}, u32[]{:S(2)}) copy-start(s32[4]{0:T(128)} %dest_ref.1) | copy-start | bytes 52
  12.1 0.7 %copy-start.6 = (f32[4]{0:T(128)S(1)}, f32[4]{0:T(128)}, u32[]{:S(2)}) copy-start(f32[4]{0:T(128)} %weight_ref.1) | copy-start | bytes 52
  13.4 29.9 %collective-permute-start.2 = (f32[168,128]{1,0:T(8,128)S(1)}, f32[168,128]{1,0:T(8,128)S(1)}, u32[]{:S(2)}, u32[]{:S(2)}) collective-permute-start(f32[168,128]{1,0:T(8,128)S(1)} %shard_map.77.refs_0_), channel_id=1, source_target_pairs={{0,4},{1,13},{2,6},{3,15},{4,8},{5,1},{6,10},{7,3},{8,12},{9,5},{1... | collective-permute-start | bytes 258056 | tf_op jit(solution)/shard_map/ppermute | solution.py:253
  20.6 22.7 %collective-permute-start.1 = (f32[168,128]{1,0:T(8,128)S(1)}, f32[168,128]{1,0:T(8,128)S(1)}, u32[]{:S(2)}, u32[]{:S(2)}) collective-permute-start(f32[168,128]{1,0:T(8,128)S(1)} %shard_map.77.refs_0_), channel_id=1, source_target_pairs={{0,12},{1,5},{2,14},{3,7},{4,0},{5,9},{6,2},{7,11},{8,4},{9,13},{1... | collective-permute-start | bytes 258056 | tf_op jit(solution)/shard_map/ppermute | solution.py:253
  26.2 19.9 %collective-permute-start = (f32[168,128]{1,0:T(8,128)S(1)}, f32[168,128]{1,0:T(8,128)S(1)}, u32[]{:S(2)}, u32[]{:S(2)}) collective-permute-start(f32[168,128]{1,0:T(8,128)S(1)} %shard_map.77.refs_0_), channel_id=1, source_target_pairs={{0,7},{1,10},{2,9},{3,12},{4,11},{5,14},{6,13},{7,0},{8,15},{9,2},... | collective-permute-start | bytes 258056 | tf_op jit(solution)/shard_map/ppermute | solution.py:253
  35.9 25.8 %all-to-all-start.1 = ((f32[32,24,128]{2,1,0:T(8,128)}), f32[32,24,128]{2,1,0:T(8,128)S(1)}, u32[]{:S(2)}, u32[]{:S(2)}) async-start(f32[32,24,128]{2,1,0:T(8,128)} %bitcast.6), calls=%async_computation.1 | async-start | bytes 786432 | tf_op jit(solution)/shard_map/all_to_all | solution.py:301
  46.1 11.7 %copy-start.3 = (f32[2048]{0:T(1024)S(1)}, f32[2048]{0:T(1024)}, u32[]{:S(2)}) copy-start(f32[2048]{0:T(1024)} %param.7) | copy-start | bytes 24580
  47.4 10.5 %collective-permute-start.3 = (f32[328,128]{1,0:T(8,128)S(1)}, f32[328,128]{1,0:T(8,128)S(1)}, u32[]{:S(2)}, u32[]{:S(2)}) collective-permute-start(f32[328,128]{1,0:T(8,128)S(1)} %get-tuple-element.5), channel_id=1, source_target_pairs={{0,15},{1,2},{2,1},{3,4},{4,3},{5,6},{6,5},{7,8},{8,7},{9,10},{10,... | collective-permute-start | bytes 503816 | tf_op jit(solution)/shard_map/ppermute | solution.py:253
  49.7 8.1 %collective-permute-start.4 = (f32[328,128]{1,0:T(8,128)S(1)}, f32[328,128]{1,0:T(8,128)S(1)}, u32[]{:S(2)}, u32[]{:S(2)}) collective-permute-start(f32[328,128]{1,0:T(8,128)S(1)} %get-tuple-element.6), channel_id=1, source_target_pairs={{0,1},{1,0},{2,3},{3,2},{4,5},{5,4},{6,7},{7,6},{8,9},{9,8},{10,11... | collective-permute-start | bytes 503816 | tf_op jit(solution)/shard_map/ppermute | solution.py:253
  53.6 8.2 %collective-permute-start.5 = (f32[328,128]{1,0:T(8,128)S(1)}, f32[328,128]{1,0:T(8,128)S(1)}, u32[]{:S(2)}, u32[]{:S(2)}) collective-permute-start(f32[328,128]{1,0:T(8,128)S(1)} %get-tuple-element.7), channel_id=1, source_target_pairs={{0,14},{1,3},{2,0},{3,5},{4,2},{5,7},{6,4},{7,9},{8,6},{9,11},{10,... | collective-permute-start | bytes 503816 | tf_op jit(solution)/shard_map/ppermute | solution.py:253

commit v4 on v3

--- a/solution.py
+++ b/solution.py
@@ -10,7 +10,7 @@
 LANES = 128
 ROWS = 8
 META = 8
-OWNER_AT, DEST_AT = 16, 24
+OWNER_AT, DEST_AT, USED_AT = 16, 24, 40
 VMEM = 32 * 1024 * 1024
 SLOW = 20_000_000_000
 CAP = 2
@@ -64,7 +64,7 @@
 
 def weigh_kernel(owner_ref, dest_ref, weight_ref, flow_ref, rotor_ref, mine_ref):
     nvars, _, cells = flow_ref.shape
-    faces = weight_ref.shape[0]
+    faces = weight_ref.shape[1]
     block = nvars * ROWS
     lane = lax.broadcasted_iota(jnp.int32, (ROWS, LANES), 1)
     meta = jnp.zeros((ROWS, LANES), jnp.float32)
@@ -74,32 +74,40 @@
         meta = jnp.where(lane == v, tail, meta)
         meta = jnp.where(lane == nvars + v, head, meta)
     for f in range(faces):
-        meta = jnp.where(lane == OWNER_AT + f, owner_ref[f].astype(jnp.float32), meta)
-        meta = jnp.where(lane == DEST_AT + f, dest_ref[f].astype(jnp.float32), meta)
+        own = slice(f, f + 1)
+        weight = jnp.broadcast_to(weight_ref[:, own], (ROWS, LANES))
+        for at, ref in ((OWNER_AT, owner_ref), (DEST_AT, dest_ref)):
+            meta = jnp.where(lane == at + f, ref[:, own].astype(jnp.float32), meta)
         for v in range(nvars):
             rows = rotor_ref[pl.ds(v * faces + f, ROWS, stride=nvars * faces), :]
             at = f * block + v * ROWS
-            mine_ref[at : at + ROWS, :] = weight_ref[f] * rows
+            mine_ref[at : at + ROWS, :] = weight * rows
     mine_ref[faces * block :, :] = meta
 
 
-def route(items, target, halo, block, out_ref):
+def route(items, targets, halo, block, out_refs):
     lane = lax.broadcasted_iota(jnp.int32, (META, LANES), 1)
-    slots = (out_ref.shape[0] - META) // block
-    meta = jnp.where(lane < OWNER_AT, halo, -1.0)
-    used = jnp.int32(0)
+    metas = [jnp.where(lane < OWNER_AT, halo, -1.0) for _ in targets]
+    used = [jnp.int32(0) for _ in targets]
     for ref, at, owner, dest in items:
-        hit = owner == target
-
-        @pl.when(hit)
-        def _(ref=ref, at=at, used=used):
-            to = pl.multiple_of(used * block, block)
-            out_ref[pl.ds(to, block), :] = ref[at : at + block, :]
-
-        where = jnp.where(hit, DEST_AT + used, -1)
-        meta = jnp.where(lane == where, dest.astype(jnp.float32), meta)
-        used = used + hit.astype(jnp.int32)
-    out_ref[slots * block :, :] = meta
+        hits = [owner == target for target in targets]
+
+        @pl.when(functools.reduce(jnp.logical_or, hits))
+        def _(ref=ref, at=at, hits=hits, used=tuple(used)):
+            for hit, slot, out_ref in zip(hits, used, out_refs):
+
+                @pl.when(hit)
+                def _(slot=slot, out_ref=out_ref):
+                    to = pl.multiple_of(slot * block, block)
+                    out_ref[pl.ds(to, block), :] = ref[at : at + block, :]
+
+        for i, hit in enumerate(hits):
+            where = jnp.where(hit, DEST_AT + used[i], -1)
+            metas[i] = jnp.where(lane == where, dest.astype(jnp.float32), metas[i])
+            used[i] = used[i] + hit.astype(jnp.int32)
+    for meta, count, out_ref in zip(metas, used, out_refs):
+        meta = jnp.where(lane == USED_AT, count.astype(jnp.float32), meta)
+        out_ref[out_ref.shape[0] - META :, :] = meta
 
 
 def fetch_ids(parts, ids_ref, sems):
@@ -126,7 +134,8 @@
 
 
 def far_hops(plane):
-    return [side(plane) * by for by in (-7, 4, -4)]
+    pair = 4 - 8 * (plane // 4 % 2)
+    return [pair, -pair, -7 * side(plane)]
 
 
 def near_hops(plane):
@@ -153,15 +162,15 @@
     count = lax.axis_size("pitch")
     halo = held[0][held[0].shape[0] - META :, :]
     items = blocks_of(held, block, ids_ref)
-    for by, out_ref in zip(near_hops(me), out_refs):
-        route(items, lax.rem(me + count + by, count), halo, block, out_ref)
+    targets = [lax.rem(me + count + by, count) for by in near_hops(me)]
+    route(items, targets, halo, block, out_refs)
 
 
 def add_block(out_ref, ref, at, dest):
     nvars = out_ref.shape[0]
     to = pl.ds(pl.multiple_of(dest * LANES, LANES), LANES)
     for v in range(nvars):
-        out_ref[v, :, to] += ref[at + v * ROWS : at + (v + 1) * ROWS, :]
+        out_ref[v, :, to] += ref[pl.ds(pl.multiple_of(at + v * ROWS, ROWS), ROWS), :]
 
 
 def base_kernel(flow_ref, speed_ref, first_ref, second_ref, *refs):
@@ -240,12 +249,12 @@
         mean_ref[v : v + 1, at] = cells_ref[row : row + 1, :]
     wait()
     for i, ref in enumerate(blocks):
-        for slot in range((ref.shape[0] - META) // block):
-            dest = ids_ref[i, 0, DEST_AT + slot].astype(jnp.int32)
-
-            @pl.when(dest >= 0)
-            def _(ref=ref, slot=slot, dest=dest):
-                add_block(out_ref, ref, slot * block, dest)
+
+        def add(slot, carry, i=i, ref=ref):
+            add_block(out_ref, ref, slot * block, ids_ref[i, 0, DEST_AT + slot].astype(jnp.int32))
+            return carry
+
+        lax.fori_loop(0, ids_ref[i, 0, USED_AT].astype(jnp.int32), add, 0)
 
 
 def sent_by(array, hops, i):
@@ -261,7 +270,7 @@
     block = nvars * inst
     tiles = nvars * cells // LANES
     slots = -(-(tiles + tiles // ROWS) // devs)
-    owner = owner.reshape(faces)
+    owner, dest_block, intersection = [a.reshape(1, faces) for a in (owner, dest_block, intersection)]
     rotor = jnp.transpose(rotor_face, (0, 2, 1, 3)).reshape(inst * nvars * faces, LANES)
     speed = speed.reshape(cells // LANES, LANES)
 
@@ -269,7 +278,7 @@
     mine = call(
         weigh_kernel,
         f32(faces * block + META, LANES),
-        [smem(), smem(), smem(), vmem(), vmem()],
+        [vmem()] * 5,
         moved=600_000,
     )(owner, dest_block, intersection, flow, rotor)
     by_cell = lax.all_to_all(packed, "tm", 0, 0, tiled=True)

time: 64 us -> 62.3 us (0.973)
  the two profiles are of different devices: /device:TPU:2 before, /device:TPU:34 now
where the time goes in v4:
time: 62.3 us; the launch traced here: 61.8 us
  starting transfers between devices  46.5 us (75%)
  waiting for transfers between devices  6.49 us (10%)
  Pallas kernels  6.4 us (10%)
  local copies, waits for them, and re-layouts  1.63 us (3%)
  between operations  0.82 us (1%)
    ppermute x6, starting transfers between devices, sent_by(): lax.ppermute(array, 'pitch', [(p, (p + hops(p)[i]) % count) for p in rang...  31.3 us
    all_to_all x1, starting transfers between devices, per_device(): by_cell = lax.all_to_all(packed, 'tm', 0, 0, tiled=True)  7.75 us
    all_to_all x1, starting transfers between devices, per_device(): by_time = lax.all_to_all(product, 'tm', 0, 0, tiled=True)  7.38 us
    ppermute x6, waiting for transfers between devices, sent_by(): lax.ppermute(array, 'pitch', [(p, (p + hops(p)[i]) % count) for p in rang...  6.49 us
    pallas_call x1, Pallas kernels, per_device(): call(finish_kernel, (f32(nvars, inst, cells), f32(nvars, cells)), [vmem()...  1.74 us
    unnamed x14, local copies, waits for them, and re-layouts  1.63 us
    pallas_call x1, Pallas kernels, per_device(): call(functools.partial(spectral_kernel, count=count, first_mean=tiles, la...  1.44 us
  transfers between devices with their start and end apart: 8, of which 2 were waited for; matrix products, arithmetic and copies ran while one was open for 0% of the time, Pallas kernels for 6%

profile of v4, /device:TPU:34, one launch (start us, length us, event | category | flops | bytes accessed | tf_op | source)
XLA Modules:
  0.0 61.8 jit_solution(7812928079815029972)
XLA Ops:
  0.6 0.0 copy-start
  0.6 1.0 %copy-done = f32[5,8,2048]{2,1,0:T(8,128)S(1)} copy-done((f32[5,8,2048]{2,1,0:T(8,128)S(1)}, f32[5,8,2048]{2,1,0:T(8,128)}, u32[]{:S(2)}) %copy-start) | copy-done | bytes 327704
  1.6 0.8 %shard_map.80 = f32[768,128]{1,0:T(8,128)} custom-call(f32[5,8,2048]{2,1,0:T(8,128)S(1)} %copy-done), custom_call_target="tpu_custom_call" | custom-call | bytes 700000 | tf_op jit(solution)/shard_map/pallas_call | solution.py:277
  2.5 7.8 %all-to-all-start = ((f32[32,24,128]{2,1,0:T(8,128)}), f32[32,24,128]{2,1,0:T(8,128)S(1)}, u32[]{:S(2)}, u32[]{:S(2)}) async-start(f32[32,24,128]{2,1,0:T(8,128)} %bitcast.6), calls=%async_computation | async-start | bytes 786432 | tf_op jit(solution)/shard_map/all_to_all | solution.py:284
  10.2 0.0 copy-start.4
  10.2 0.0 copy-start.5
  10.2 0.0 copy-start.6
  10.2 0.0 copy-done.1
  10.3 0.6 copy-done.4
  10.9 0.0 copy-done.5
  10.9 0.0 copy-done.6
  10.9 0.1 shard_map.77.refs_0_
  11.0 14.4 %collective-permute-start.2 = (f32[168,128]{1,0:T(8,128)S(1)}, f32[168,128]{1,0:T(8,128)S(1)}, u32[]{:S(2)}, u32[]{:S(2)}) collective-permute-start(f32[168,128]{1,0:T(8,128)S(1)} %shard_map.77.refs_0_), channel_id=1, source_target_pairs={{0,7},{1,10},{2,9},{3,12},{4,11},{5,14},{6,13},{7,0},{8,15},{9,2},... | collective-permute-start | bytes 258056 | tf_op jit(solution)/shard_map/ppermute | solution.py:262
  25.4 2.5 %collective-permute-start.1 = (f32[168,128]{1,0:T(8,128)S(1)}, f32[168,128]{1,0:T(8,128)S(1)}, u32[]{:S(2)}, u32[]{:S(2)}) collective-permute-start(f32[168,128]{1,0:T(8,128)S(1)} %shard_map.77.refs_0_), channel_id=1, source_target_pairs={{0,12},{1,13},{2,14},{3,15},{4,8},{5,9},{6,10},{7,11},{8,4},{9,5},... | collective-permute-start | bytes 258056 | tf_op jit(solution)/shard_map/ppermute | solution.py:262
  27.8 3.8 %collective-permute-start = (f32[168,128]{1,0:T(8,128)S(1)}, f32[168,128]{1,0:T(8,128)S(1)}, u32[]{:S(2)}, u32[]{:S(2)}) collective-permute-start(f32[168,128]{1,0:T(8,128)S(1)} %shard_map.77.refs_0_), channel_id=1, source_target_pairs={{0,4},{1,5},{2,6},{3,7},{4,0},{5,1},{6,2},{7,3},{8,12},{9,13},{10,... | collective-permute-start | bytes 258056 | tf_op jit(solution)/shard_map/ppermute | solution.py:262
  31.6 0.0 all-to-all-done
  31.6 1.4 %shard_map.81 = f32[768,128]{1,0:T(8,128)} custom-call(f32[768,128]{1,0:T(8,128)S(1)} %bitcast.12), custom_call_target="tpu_custom_call" | custom-call | flops 301989888 | bytes 1000000 | tf_op jit(solution)/shard_map/pallas_call | solution.py:285
  33.1 7.4 %all-to-all-start.1 = ((f32[32,24,128]{2,1,0:T(8,128)}), f32[32,24,128]{2,1,0:T(8,128)S(1)}, u32[]{:S(2)}, u32[]{:S(2)}) async-start(f32[32,24,128]{2,1,0:T(8,128)} %bitcast.8), calls=%async_computation.1 | async-start | bytes 786432 | tf_op jit(solution)/shard_map/all_to_all | solution.py:310
  40.5 0.0 collective-permute-done.2.refs_3_
  40.5 0.0 collective-permute-done.1.refs_2_
  40.5 0.0 collective-permute-done.refs_1_
  40.5 0.0 copy-start.3
  40.5 1.2 %shard_map.78 = (f32[328,128]{1,0:T(8,128)S(1)}, f32[328,128]{1,0:T(8,128)S(1)}, f32[328,128]{1,0:T(8,128)S(1)}) custom-call(f32[168,128]{1,0:T(8,128)S(1)} %shard_map.77.refs_0_, f32[168,128]{1,0:T(8,128)S(1)} %collective-permute-done.refs_1_, f32[168,128]{1,0:T(8,128)S(1)} %collective-permute-done.1.refs_2_, f32[168,128]{1,0:T(8,128)S(1)} %collective-permute-done.2.refs_3_), custom_call_target="tpu_custom_call" | custom-call | flops 20000000000 | bytes 1500000 | tf_op jit(solution)/shard_map/pallas_call | solution.py:293
  41.7 3.0 %collective-permute-start.3 = (f32[328,128]{1,0:T(8,128)S(1)}, f32[328,128]{1,0:T(8,128)S(1)}, u32[]{:S(2)}, u32[]{:S(2)}) collective-permute-start(f32[328,128]{1,0:T(8,128)S(1)} %get-tuple-element.5), channel_id=1, source_target_pairs={{0,15},{1,2},{2,1},{3,4},{4,3},{5,6},{6,5},{7,8},{8,7},{9,10},{10,... | collective-permute-start | bytes 503816 | tf_op jit(solution)/shard_map/ppermute | solution.py:262
  44.7 4.3 %collective-permute-start.4 = (f32[328,128]{1,0:T(8,128)S(1)}, f32[328,128]{1,0:T(8,128)S(1)}, u32[]{:S(2)}, u32[]{:S(2)}) collective-permute-start(f32[328,128]{1,0:T(8,128)S(1)} %get-tuple-element.6), channel_id=1, source_target_pairs={{0,1},{1,0},{2,3},{3,2},{4,5},{5,4},{6,7},{7,6},{8,9},{9,8},{10,11... | collective-permute-start | bytes 503816 | tf_op jit(solution)/shard_map/ppermute | solution.py:262
  49.0 3.5 %collective-permute-start.5 = (f32[328,128]{1,0:T(8,128)S(1)}, f32[328,128]{1,0:T(8,128)S(1)}, u32[]{:S(2)}, u32[]{:S(2)}) collective-permute-start(f32[328,128]{1,0:T(8,128)S(1)} %get-tuple-element.7), channel_id=1, source_target_pairs={{0,14},{1,3},{2,0},{3,5},{4,2},{5,7},{6,4},{7,9},{8,6},{9,11},{10,... | collective-permute-start | bytes 503816 | tf_op jit(solution)/shard_map/ppermute | solution.py:262
  52.4 0.0 collective-permute-done.3.first_ref.refs_2_
  52.4 3.9 %collective-permute-done.4.second_ref.refs_3_ = f32[328,128]{1,0:T(8,128)S(1)} collective-permute-done((f32[328,128]{1,0:T(8,128)S(1)}, f32[328,128]{1,0:T(8,128)S(1)}, u32[]{:S(2)}, u32[]{:S(2)}) %collective-permute-start.4) | collective-permute-done | bytes 167968 | tf_op jit(solution)/shard_map/ppermute | solution.py:262
  56.4 1.1 %shard_map.79.refs_0_ = f32[5,8,2048]{2,1,0:T(8,128)S(1)} custom-call(f32[5,8,2048]{2,1,0:T(8,128)S(1)} %copy-done.1, f32[16,128]{1,0:T(8,128)S(1)} %bitcast.14, f32[328,128]{1,0:T(8,128)S(1)} %collective-permute-done.3.first_ref.refs_2_, f32[328,128]{1,0:T(8,128)S(1)} %collective-permute-done.4.second_ref.refs_3_, f32[168,128]{1,0:T(8,128)S(1)} %shard_map.77.refs_0_, ...), custom_call_target="tpu_custom_call" | custom-call | bytes 900000 | tf_op jit(solution)/shard_map/pallas_call | solution.py:302
  57.5 2.6 %collective-permute-done.5.refs_4_ = f32[328,128]{1,0:T(8,128)S(1)} collective-permute-done((f32[328,128]{1,0:T(8,128)S(1)}, f32[328,128]{1,0:T(8,128)S(1)}, u32[]{:S(2)}, u32[]{:S(2)}) %collective-permute-start.5) | collective-permute-done | bytes 167968 | tf_op jit(solution)/shard_map/ppermute | solution.py:262
  60.0 0.0 all-to-all-done.1
  60.0 1.7 %shard_map.82 = (f32[5,8,2048]{2,1,0:T(8,128)}, f32[5,2048]{1,0:T(8,128)}) custom-call(f32[5,8,2048]{2,1,0:T(8,128)S(1)} %shard_map.79.refs_0_, f32[768,128]{1,0:T(8,128)S(1)} %bitcast.11, f32[328,128]{1,0:T(8,128)S(1)} %collective-permute-done.3.first_ref.refs_2_, f32[328,128]{1,0:T(8,128)S(1)} %collective-permute-done.4.second_ref.refs_3_, ...), custom_call_target="tpu_custom_call" | custom-call | bytes 1500000 | tf_op jit(solution)/shard_map/pallas_call | solution.py:311
  (4 shorter events, 0.0 us)
Async XLA Ops:
  0.6 1.0 %copy-start = (f32[5,8,2048]{2,1,0:T(8,128)S(1)}, f32[5,8,2048]{2,1,0:T(8,128)}, u32[]{:S(2)}) copy-start(f32[5,8,2048]{2,1,0:T(8,128)} %flow_ref.5) | copy-start | bytes 983044
  2.4 7.8 %copy-start.1 = (f32[5,8,2048]{2,1,0:T(8,128)S(1)}, f32[5,8,2048]{2,1,0:T(8,128)}, u32[]{:S(2)}) copy-start(f32[5,8,2048]{2,1,0:T(8,128)} %flow_ref.5) | copy-start | bytes 983044
  2.5 7.8 %copy-start.2 = (f32[8,4,5,128]{3,1,2,0:T(4,128)S(1)}, f32[8,4,5,128]{3,1,2,0:T(4,128)}, u32[]{:S(2)}) copy-start(f32[8,4,5,128]{3,1,2,0:T(4,128)} %param.8) | copy-start | bytes 245764
  2.5 29.2 %all-to-all-start = ((f32[32,24,128]{2,1,0:T(8,128)}), f32[32,24,128]{2,1,0:T(8,128)S(1)}, u32[]{:S(2)}, u32[]{:S(2)}) async-start(f32[32,24,128]{2,1,0:T(8,128)} %bitcast.6), calls=%async_computation | async-start | bytes 786432 | tf_op jit(solution)/shard_map/all_to_all | solution.py:284
  10.2 0.7 %copy-start.4 = (s32[4,1]{0,1:T(1,128)S(1)}, s32[4,1]{0,1:T(1,128)}, u32[]{:S(2)}) copy-start(s32[4,1]{0,1:T(1,128)} %param.9) | copy-start | bytes 52
  10.2 0.7 %copy-start.5 = (s32[4]{0:T(128)S(1)}, s32[4]{0:T(128)}, u32[]{:S(2)}) copy-start(s32[4]{0:T(128)} %param.10) | copy-start | bytes 52
  10.2 0.7 %copy-start.6 = (f32[4]{0:T(128)S(1)}, f32[4]{0:T(128)}, u32[]{:S(2)}) copy-start(f32[4]{0:T(128)} %param.11) | copy-start | bytes 52
  11.0 29.5 %collective-permute-start.2 = (f32[168,128]{1,0:T(8,128)S(1)}, f32[168,128]{1,0:T(8,128)S(1)}, u32[]{:S(2)}, u32[]{:S(2)}) collective-permute-start(f32[168,128]{1,0:T(8,128)S(1)} %shard_map.77.refs_0_), channel_id=1, source_target_pairs={{0,7},{1,10},{2,9},{3,12},{4,11},{5,14},{6,13},{7,0},{8,15},{9,2},... | collective-permute-start | bytes 258056 | tf_op jit(solution)/shard_map/ppermute | solution.py:262
  25.4 15.1 %collective-permute-start.1 = (f32[168,128]{1,0:T(8,128)S(1)}, f32[168,128]{1,0:T(8,128)S(1)}, u32[]{:S(2)}, u32[]{:S(2)}) collective-permute-start(f32[168,128]{1,0:T(8,128)S(1)} %shard_map.77.refs_0_), channel_id=1, source_target_pairs={{0,12},{1,13},{2,14},{3,15},{4,8},{5,9},{6,10},{7,11},{8,4},{9,5},... | collective-permute-start | bytes 258056 | tf_op jit(solution)/shard_map/ppermute | solution.py:262
  27.8 12.6 %collective-permute-start = (f32[168,128]{1,0:T(8,128)S(1)}, f32[168,128]{1,0:T(8,128)S(1)}, u32[]{:S(2)}, u32[]{:S(2)}) collective-permute-start(f32[168,128]{1,0:T(8,128)S(1)} %shard_map.77.refs_0_), channel_id=1, source_target_pairs={{0,4},{1,5},{2,6},{3,7},{4,0},{5,1},{6,2},{7,3},{8,12},{9,13},{10,... | collective-permute-start | bytes 258056 | tf_op jit(solution)/shard_map/ppermute | solution.py:262
  33.1 27.0 %all-to-all-start.1 = ((f32[32,24,128]{2,1,0:T(8,128)}), f32[32,24,128]{2,1,0:T(8,128)S(1)}, u32[]{:S(2)}, u32[]{:S(2)}) async-start(f32[32,24,128]{2,1,0:T(8,128)} %bitcast.8), calls=%async_computation.1 | async-start | bytes 786432 | tf_op jit(solution)/shard_map/all_to_all | solution.py:310
  40.5 15.9 %copy-start.3 = (f32[2048]{0:T(1024)S(1)}, f32[2048]{0:T(1024)}, u32[]{:S(2)}) copy-start(f32[2048]{0:T(1024)} %param.7) | copy-start | bytes 24580
  41.7 10.8 %collective-permute-start.3 = (f32[328,128]{1,0:T(8,128)S(1)}, f32[328,128]{1,0:T(8,128)S(1)}, u32[]{:S(2)}, u32[]{:S(2)}) collective-permute-start(f32[328,128]{1,0:T(8,128)S(1)} %get-tuple-element.5), channel_id=1, source_target_pairs={{0,15},{1,2},{2,1},{3,4},{4,3},{5,6},{6,5},{7,8},{8,7},{9,10},{10,... | collective-permute-start | bytes 503816 | tf_op jit(solution)/shard_map/ppermute | solution.py:262
  44.7 11.7 %collective-permute-start.4 = (f32[328,128]{1,0:T(8,128)S(1)}, f32[328,128]{1,0:T(8,128)S(1)}, u32[]{:S(2)}, u32[]{:S(2)}) collective-permute-start(f32[328,128]{1,0:T(8,128)S(1)} %get-tuple-element.6), channel_id=1, source_target_pairs={{0,1},{1,0},{2,3},{3,2},{4,5},{5,4},{6,7},{7,6},{8,9},{9,8},{10,11... | collective-permute-start | bytes 503816 | tf_op jit(solution)/shard_map/ppermute | solution.py:262
  49.0 11.1 %collective-permute-start.5 = (f32[328,128]{1,0:T(8,128)S(1)}, f32[328,128]{1,0:T(8,128)S(1)}, u32[]{:S(2)}, u32[]{:S(2)}) collective-permute-start(f32[328,128]{1,0:T(8,128)S(1)} %get-tuple-element.7), channel_id=1, source_target_pairs={{0,14},{1,3},{2,0},{3,5},{4,2},{5,7},{6,4},{7,9},{8,6},{9,11},{10,... | collective-permute-start | bytes 503816 | tf_op jit(solution)/shard_map/ppermute | solution.py:262

commit v5 on v4

--- a/solution.py
+++ b/solution.py
@@ -12,6 +12,8 @@
 META = 8
 OWNER_AT, DEST_AT, USED_AT = 16, 24, 40
 VMEM = 32 * 1024 * 1024
+ALL_VMEM = 60 * 1024 * 1024
+IN = 5
 SLOW = 20_000_000_000
 CAP = 2
 FAR, NEAR = 3, 3
@@ -25,14 +27,14 @@
     return pl.BlockSpec(memory_space=pltpu.SMEM)
 
 
-def call(body, outs, in_specs, scratch=(), flops=0, moved=0):
+def call(body, outs, in_specs, scratch=(), flops=0, moved=0, room=VMEM):
     return pl.pallas_call(
         body,
         out_shape=outs,
         in_specs=in_specs,
         out_specs=jax.tree.map(lambda _: vmem(), outs),
         scratch_shapes=list(scratch),
-        compiler_params=pltpu.CompilerParams(vmem_limit_bytes=VMEM),
+        compiler_params=pltpu.CompilerParams(vmem_limit_bytes=room),
         cost_estimate=pl.CostEstimate(flops=flops, bytes_accessed=moved, transcendentals=0),
     )
 
@@ -41,7 +43,21 @@
     return jax.ShapeDtypeStruct(shape, jnp.float32)
 
 
-def pack_kernel(flow_ref, out_ref):
+def prepare_kernel(*refs):
+    given, (packed_ref, mine_ref), held, sems = refs[:IN], refs[IN : IN + 2], refs[IN + 2 : -1], refs[-1]
+    flow_ref, rotor_ref, owner_ref, dest_ref, weight_ref = held
+    nvars = flow_ref.shape[0]
+    flows = [pltpu.make_async_copy(given[0].at[v], flow_ref.at[v], sems.at[v]) for v in range(nvars)]
+    rest = [pltpu.make_async_copy(given[i], held[i], sems.at[nvars - 1 + i]) for i in range(1, IN)]
+    for copy in flows + rest:
+        copy.start()
+    pack(flows, flow_ref, packed_ref)
+    for copy in rest:
+        copy.wait()
+    weigh(owner_ref, dest_ref, weight_ref, flow_ref, rotor_ref, mine_ref)
+
+
+def pack(copies, flow_ref, out_ref):
     nvars, _, cells = flow_ref.shape
     per = cells // LANES
     tiles = nvars * per
@@ -49,6 +65,8 @@
     sums = None
     for m in range(tiles):
         v, c = divmod(m, per)
+        if c == 0:
+            copies[v].wait()
         tile = flow_ref[v, :, c * LANES : (c + 1) * LANES]
         out_ref[m * ROWS : (m + 1) * ROWS, :] = tile
         total = jnp.sum(tile, axis=0, keepdims=True)
@@ -58,11 +76,10 @@
             q = tiles + m // ROWS
             out_ref[q * ROWS : (q + 1) * ROWS, :] = sums
     used = (tiles + tiles // ROWS) * ROWS
-    rest = out_ref.shape[0] - used
-    out_ref[used:, :] = jnp.zeros((rest, LANES), jnp.float32)
-
-
-def weigh_kernel(owner_ref, dest_ref, weight_ref, flow_ref, rotor_ref, mine_ref):
+    out_ref[used:, :] = jnp.zeros((out_ref.shape[0] - used, LANES), jnp.float32)
+
+
+def weigh(owner_ref, dest_ref, weight_ref, flow_ref, rotor_ref, mine_ref):
     nvars, _, cells = flow_ref.shape
     faces = weight_ref.shape[1]
     block = nvars * ROWS
@@ -274,13 +291,15 @@
     rotor = jnp.transpose(rotor_face, (0, 2, 1, 3)).reshape(inst * nvars * faces, LANES)
     speed = speed.reshape(cells // LANES, LANES)
 
-    packed = call(pack_kernel, f32(devs * slots * ROWS, LANES), [vmem()], moved=700_000)(flow)
-    mine = call(
-        weigh_kernel,
-        f32(faces * block + META, LANES),
-        [vmem()] * 5,
-        moved=600_000,
-    )(owner, dest_block, intersection, flow, rotor)
+    operands = (flow, rotor, owner, dest_block, intersection)
+    packed, mine = call(
+        prepare_kernel,
+        (f32(devs * slots * ROWS, LANES), f32(faces * block + META, LANES)),
+        [pl.BlockSpec(memory_space=pl.ANY)] * IN,
+        [pltpu.VMEM(a.shape, a.dtype) for a in operands] + [pltpu.SemaphoreType.DMA((nvars + IN - 1,))],
+        moved=1_200_000,
+        room=ALL_VMEM,
+    )(*operands)
     by_cell = lax.all_to_all(packed, "tm", 0, 0, tiled=True)
     product = call(
         functools.partial(spectral_kernel, count=count, first_mean=tiles, last_mean=tiles + tiles // ROWS),

time: 62.3 us -> 61.4 us (0.986)
  local copies, waits for them, and re-layouts: 1.63 us -> 0.02 us
  Pallas kernels: 6.4 us -> 7.13 us
    unnamed x14 -> x6, local copies, waits for them, and re-layouts: 1.63 us -> 0.02 us
    pallas_call x2 -> x1, Pallas kernels: 0.94 us -> 1.91 us  [per_device(): call(prepare_kernel, (f32(devs * slots * ROWS, LANES), f32(faces * block...]
where the time goes in v5:
time: 61.4 us; the launch traced here: 60.9 us
  starting transfers between devices  46.5 us (76%)
  Pallas kernels  7.13 us (12%)
  waiting for transfers between devices  6.49 us (11%)
  between operations  0.79 us (1%)
    ppermute x6, starting transfers between devices, sent_by(): lax.ppermute(array, 'pitch', [(p, (p + hops(p)[i]) % count) for p in rang...  31.4 us
    all_to_all x1, starting transfers between devices, per_device(): by_cell = lax.all_to_all(packed, 'tm', 0, 0, tiled=True)  7.77 us
    all_to_all x1, starting transfers between devices, per_device(): by_time = lax.all_to_all(product, 'tm', 0, 0, tiled=True)  7.38 us
    ppermute x6, waiting for transfers between devices, sent_by(): lax.ppermute(array, 'pitch', [(p, (p + hops(p)[i]) % count) for p in rang...  6.48 us
    pallas_call x1, Pallas kernels, per_device(): call(prepare_kernel, (f32(devs * slots * ROWS, LANES), f32(faces * block...  1.91 us
    pallas_call x1, Pallas kernels, per_device(): call(finish_kernel, (f32(nvars, inst, cells), f32(nvars, cells)), [vmem()...  1.55 us
    pallas_call x1, Pallas kernels, per_device(): call(functools.partial(spectral_kernel, count=count, first_mean=tiles, la...  1.43 us
  transfers between devices with their start and end apart: 8, of which 2 were waited for; matrix products, arithmetic and copies ran while one was open for 0% of the time, Pallas kernels for 6%

profile of v5, /device:TPU:34, one launch (start us, length us, event | category | flops | bytes accessed | tf_op | source)
XLA Modules:
  0.0 60.9 jit_solution(6606402011176959)
XLA Ops:
  0.6 1.9 %shard_map.77 = (f32[768,128]{1,0:T(8,128)}, f32[168,128]{1,0:T(8,128)}) custom-call(f32[5,8,2048]{2,1,0:T(8,128)} %flow_ref.1, f32[160,128]{1,0:T(8,128)} %bitcast.15, s32[1,4]{1,0:T(1,128)} %bitcast.16, s32[1,4]{1,0:T(1,128)} %bitcast.17, f32[1,4]{1,0:T(1,128)} %bitcast.18), custom_call_target="tpu_custom_call" | custom-call | bytes 1200000 | tf_op jit(solution)/shard_map/pallas_call | solution.py:295
  2.5 0.0 copy-start.1
  2.6 7.8 %all-to-all-start = ((f32[32,24,128]{2,1,0:T(8,128)}), f32[32,24,128]{2,1,0:T(8,128)S(1)}, u32[]{:S(2)}, u32[]{:S(2)}) async-start(f32[32,24,128]{2,1,0:T(8,128)} %bitcast.14), calls=%async_computation | async-start | bytes 786432 | tf_op jit(solution)/shard_map/all_to_all | solution.py:303
  10.3 0.0 copy-done.1
  10.3 14.4 %collective-permute-start.2 = (f32[168,128]{1,0:T(8,128)S(1)}, f32[168,128]{1,0:T(8,128)S(1)}, u32[]{:S(2)}, u32[]{:S(2)}) collective-permute-start(f32[168,128]{1,0:T(8,128)S(1)} %copy-done.1), channel_id=1, source_target_pairs={{0,7},{1,10},{2,9},{3,12},{4,11},{5,14},{6,13},{7,0},{8,15},{9,2},... | collective-permute-start | bytes 258056 | tf_op jit(solution)/shard_map/ppermute | solution.py:279
  24.7 2.5 %collective-permute-start.1 = (f32[168,128]{1,0:T(8,128)S(1)}, f32[168,128]{1,0:T(8,128)S(1)}, u32[]{:S(2)}, u32[]{:S(2)}) collective-permute-start(f32[168,128]{1,0:T(8,128)S(1)} %copy-done.1), channel_id=1, source_target_pairs={{0,12},{1,13},{2,14},{3,15},{4,8},{5,9},{6,10},{7,11},{8,4},{9,5},... | collective-permute-start | bytes 258056 | tf_op jit(solution)/shard_map/ppermute | solution.py:279
  27.2 3.8 %collective-permute-start = (f32[168,128]{1,0:T(8,128)S(1)}, f32[168,128]{1,0:T(8,128)S(1)}, u32[]{:S(2)}, u32[]{:S(2)}) collective-permute-start(f32[168,128]{1,0:T(8,128)S(1)} %copy-done.1), channel_id=1, source_target_pairs={{0,4},{1,5},{2,6},{3,7},{4,0},{5,1},{6,2},{7,3},{8,12},{9,13},{10,... | collective-permute-start | bytes 258056 | tf_op jit(solution)/shard_map/ppermute | solution.py:279
  31.0 0.0 all-to-all-done
  31.0 1.4 %shard_map.80 = f32[768,128]{1,0:T(8,128)} custom-call(f32[768,128]{1,0:T(8,128)S(1)} %bitcast.12), custom_call_target="tpu_custom_call" | custom-call | flops 301989888 | bytes 1000000 | tf_op jit(solution)/shard_map/pallas_call | solution.py:304
  32.4 7.4 %all-to-all-start.1 = ((f32[32,24,128]{2,1,0:T(8,128)}), f32[32,24,128]{2,1,0:T(8,128)S(1)}, u32[]{:S(2)}, u32[]{:S(2)}) async-start(f32[32,24,128]{2,1,0:T(8,128)} %bitcast.8), calls=%async_computation.1 | async-start | bytes 786432 | tf_op jit(solution)/shard_map/all_to_all | solution.py:329
  39.8 0.0 copy-start
  39.8 0.0 collective-permute-done.2.refs_3_
  39.8 0.0 collective-permute-done.1.refs_2_
  39.8 0.0 collective-permute-done.refs_1_
  39.8 0.0 copy-start.2
  39.8 1.1 %shard_map.78 = (f32[328,128]{1,0:T(8,128)S(1)}, f32[328,128]{1,0:T(8,128)S(1)}, f32[328,128]{1,0:T(8,128)S(1)}) custom-call(f32[168,128]{1,0:T(8,128)S(1)} %copy-done.1, f32[168,128]{1,0:T(8,128)S(1)} %collective-permute-done.refs_1_, f32[168,128]{1,0:T(8,128)S(1)} %collective-permute-done.1.refs_2_, f32[168,128]{1,0:T(8,128)S(1)} %collective-permute-done.2.refs_3_), custom_call_target="tpu_custom_call" | custom-call | flops 20000000000 | bytes 1500000 | tf_op jit(solution)/shard_map/pallas_call | solution.py:312
  41.0 2.9 %collective-permute-start.3 = (f32[328,128]{1,0:T(8,128)S(1)}, f32[328,128]{1,0:T(8,128)S(1)}, u32[]{:S(2)}, u32[]{:S(2)}) collective-permute-start(f32[328,128]{1,0:T(8,128)S(1)} %get-tuple-element.8), channel_id=1, source_target_pairs={{0,15},{1,2},{2,1},{3,4},{4,3},{5,6},{6,5},{7,8},{8,7},{9,10},{10,... | collective-permute-start | bytes 503816 | tf_op jit(solution)/shard_map/ppermute | solution.py:279
  43.9 4.3 %collective-permute-start.4 = (f32[328,128]{1,0:T(8,128)S(1)}, f32[328,128]{1,0:T(8,128)S(1)}, u32[]{:S(2)}, u32[]{:S(2)}) collective-permute-start(f32[328,128]{1,0:T(8,128)S(1)} %get-tuple-element.9), channel_id=1, source_target_pairs={{0,1},{1,0},{2,3},{3,2},{4,5},{5,4},{6,7},{7,6},{8,9},{9,8},{10,11... | collective-permute-start | bytes 503816 | tf_op jit(solution)/shard_map/ppermute | solution.py:279
  48.3 3.5 %collective-permute-start.5 = (f32[328,128]{1,0:T(8,128)S(1)}, f32[328,128]{1,0:T(8,128)S(1)}, u32[]{:S(2)}, u32[]{:S(2)}) collective-permute-start(f32[328,128]{1,0:T(8,128)S(1)} %get-tuple-element.11), channel_id=1, source_target_pairs={{0,14},{1,3},{2,0},{3,5},{4,2},{5,7},{6,4},{7,9},{8,6},{9,11},{10,... | collective-permute-start | bytes 503816 | tf_op jit(solution)/shard_map/ppermute | solution.py:279
  51.8 0.0 collective-permute-done.3.first_ref.refs_2_
  51.8 3.8 %collective-permute-done.4.second_ref.refs_3_ = f32[328,128]{1,0:T(8,128)S(1)} collective-permute-done((f32[328,128]{1,0:T(8,128)S(1)}, f32[328,128]{1,0:T(8,128)S(1)}, u32[]{:S(2)}, u32[]{:S(2)}) %collective-permute-start.4) | collective-permute-done | bytes 167968 | tf_op jit(solution)/shard_map/ppermute | solution.py:279
  55.6 0.0 copy-done
  55.6 0.0 copy-done.2
  55.6 1.1 %shard_map.79.refs_0_ = f32[5,8,2048]{2,1,0:T(8,128)S(1)} custom-call(f32[5,8,2048]{2,1,0:T(8,128)S(1)} %copy-done, f32[16,128]{1,0:T(8,128)S(1)} %bitcast.13, f32[328,128]{1,0:T(8,128)S(1)} %collective-permute-done.3.first_ref.refs_2_, f32[328,128]{1,0:T(8,128)S(1)} %collective-permute-done.4.second_ref.refs_3_, f32[168,128]{1,0:T(8,128)S(1)} %copy-done.1, ...), custom_call_target="tpu_custom_call" | custom-call | bytes 900000 | tf_op jit(solution)/shard_map/pallas_call | solution.py:321
  56.7 2.7 %collective-permute-done.5.refs_4_ = f32[328,128]{1,0:T(8,128)S(1)} collective-permute-done((f32[328,128]{1,0:T(8,128)S(1)}, f32[328,128]{1,0:T(8,128)S(1)}, u32[]{:S(2)}, u32[]{:S(2)}) %collective-permute-start.5) | collective-permute-done | bytes 167968 | tf_op jit(solution)/shard_map/ppermute | solution.py:279
  59.4 0.0 all-to-all-done.1
  59.4 1.5 %shard_map.81 = (f32[5,8,2048]{2,1,0:T(8,128)}, f32[5,2048]{1,0:T(8,128)}) custom-call(f32[5,8,2048]{2,1,0:T(8,128)S(1)} %shard_map.79.refs_0_, f32[768,128]{1,0:T(8,128)S(1)} %bitcast.11, f32[328,128]{1,0:T(8,128)S(1)} %collective-permute-done.3.first_ref.refs_2_, f32[328,128]{1,0:T(8,128)S(1)} %collective-permute-done.4.second_ref.refs_3_, ...), custom_call_target="tpu_custom_call" | custom-call | bytes 1500000 | tf_op jit(solution)/shard_map/pallas_call | solution.py:330
Async XLA Ops:
  2.5 7.8 %copy-start.1 = (f32[168,128]{1,0:T(8,128)S(1)}, f32[168,128]{1,0:T(8,128)}, u32[]{:S(2)}) copy-start(f32[168,128]{1,0:T(8,128)} %get-tuple-element.7.refs_0_) | copy-start | bytes 258052
  2.6 28.4 %all-to-all-start = ((f32[32,24,128]{2,1,0:T(8,128)}), f32[32,24,128]{2,1,0:T(8,128)S(1)}, u32[]{:S(2)}, u32[]{:S(2)}) async-start(f32[32,24,128]{2,1,0:T(8,128)} %bitcast.14), calls=%async_computation | async-start | bytes 786432 | tf_op jit(solution)/shard_map/all_to_all | solution.py:303
  10.3 29.5 %collective-permute-start.2 = (f32[168,128]{1,0:T(8,128)S(1)}, f32[168,128]{1,0:T(8,128)S(1)}, u32[]{:S(2)}, u32[]{:S(2)}) collective-permute-start(f32[168,128]{1,0:T(8,128)S(1)} %copy-done.1), channel_id=1, source_target_pairs={{0,7},{1,10},{2,9},{3,12},{4,11},{5,14},{6,13},{7,0},{8,15},{9,2},... | collective-permute-start | bytes 258056 | tf_op jit(solution)/shard_map/ppermute | solution.py:279
  24.7 15.1 %collective-permute-start.1 = (f32[168,128]{1,0:T(8,128)S(1)}, f32[168,128]{1,0:T(8,128)S(1)}, u32[]{:S(2)}, u32[]{:S(2)}) collective-permute-start(f32[168,128]{1,0:T(8,128)S(1)} %copy-done.1), channel_id=1, source_target_pairs={{0,12},{1,13},{2,14},{3,15},{4,8},{5,9},{6,10},{7,11},{8,4},{9,5},... | collective-permute-start | bytes 258056 | tf_op jit(solution)/shard_map/ppermute | solution.py:279
  27.2 12.6 %collective-permute-start = (f32[168,128]{1,0:T(8,128)S(1)}, f32[168,128]{1,0:T(8,128)S(1)}, u32[]{:S(2)}, u32[]{:S(2)}) collective-permute-start(f32[168,128]{1,0:T(8,128)S(1)} %copy-done.1), channel_id=1, source_target_pairs={{0,4},{1,5},{2,6},{3,7},{4,0},{5,1},{6,2},{7,3},{8,12},{9,13},{10,... | collective-permute-start | bytes 258056 | tf_op jit(solution)/shard_map/ppermute | solution.py:279
  32.4 27.0 %all-to-all-start.1 = ((f32[32,24,128]{2,1,0:T(8,128)}), f32[32,24,128]{2,1,0:T(8,128)S(1)}, u32[]{:S(2)}, u32[]{:S(2)}) async-start(f32[32,24,128]{2,1,0:T(8,128)} %bitcast.8), calls=%async_computation.1 | async-start | bytes 786432 | tf_op jit(solution)/shard_map/all_to_all | solution.py:329
  39.8 15.8 %copy-start = (f32[5,8,2048]{2,1,0:T(8,128)S(1)}, f32[5,8,2048]{2,1,0:T(8,128)}, u32[]{:S(2)}) copy-start(f32[5,8,2048]{2,1,0:T(8,128)} %flow_ref.1) | copy-start | bytes 983044
  39.8 15.8 %copy-start.2 = (f32[2048]{0:T(1024)S(1)}, f32[2048]{0:T(1024)}, u32[]{:S(2)}) copy-start(f32[2048]{0:T(1024)} %param.7) | copy-start | bytes 24580
  41.0 10.8 %collective-permute-start.3 = (f32[328,128]{1,0:T(8,128)S(1)}, f32[328,128]{1,0:T(8,128)S(1)}, u32[]{:S(2)}, u32[]{:S(2)}) collective-permute-start(f32[328,128]{1,0:T(8,128)S(1)} %get-tuple-element.8), channel_id=1, source_target_pairs={{0,15},{1,2},{2,1},{3,4},{4,3},{5,6},{6,5},{7,8},{8,7},{9,10},{10,... | collective-permute-start | bytes 503816 | tf_op jit(solution)/shard_map/ppermute | solution.py:279
  43.9 11.7 %collective-permute-start.4 = (f32[328,128]{1,0:T(8,128)S(1)}, f32[328,128]{1,0:T(8,128)S(1)}, u32[]{:S(2)}, u32[]{:S(2)}) collective-permute-start(f32[328,128]{1,0:T(8,128)S(1)} %get-tuple-element.9), channel_id=1, source_target_pairs={{0,1},{1,0},{2,3},{3,2},{4,5},{5,4},{6,7},{7,6},{8,9},{9,8},{10,11... | collective-permute-start | bytes 503816 | tf_op jit(solution)/shard_map/ppermute | solution.py:279
  48.3 11.1 %collective-permute-start.5 = (f32[328,128]{1,0:T(8,128)S(1)}, f32[328,128]{1,0:T(8,128)S(1)}, u32[]{:S(2)}, u32[]{:S(2)}) collective-permute-start(f32[328,128]{1,0:T(8,128)S(1)} %get-tuple-element.11), channel_id=1, source_target_pairs={{0,14},{1,3},{2,0},{3,5},{4,2},{5,7},{6,4},{7,9},{8,6},{9,11},{10,... | collective-permute-start | bytes 503816 | tf_op jit(solution)/shard_map/ppermute | solution.py:279

commit v6 on v5

--- a/solution.py
+++ b/solution.py
@@ -16,7 +16,7 @@
 IN = 5
 SLOW = 20_000_000_000
 CAP = 2
-FAR, NEAR = 3, 3
+NEAR = 3
 
 
 def vmem():
@@ -146,39 +146,42 @@
     return [pltpu.SMEM((groups, META, LANES), jnp.float32), pltpu.SemaphoreType.DMA((groups,))]
 
 
-def side(plane):
-    return 2 * (plane % 2) - 1
-
-
 def far_hops(plane):
-    pair = 4 - 8 * (plane // 4 % 2)
-    return [pair, -pair, -7 * side(plane)]
+    pair = (4 - 8 * (plane // 4 % 2)) * (1 - 2 * (plane % 2))
+    return [pair, -pair]
 
 
 def near_hops(plane):
-    return [side(plane) * by for by in (1, -1, 2)]
-
-
-def metas(refs):
-    return [(ref, ref.shape[0] - META) for ref in refs]
-
-
-def blocks_of(refs, block, ids_ref):
+    side = 2 * (plane % 2) - 1
+    return [side, -side, 2 * side]
+
+
+def metas(refs, rows=0):
+    return [(ref, at + (rows or ref.shape[0]) - META) for ref in refs for at in range(0, ref.shape[0], rows or ref.shape[0])]
+
+
+def blocks_of(refs, rows, block, ids_ref):
     items = []
-    for i, ref in enumerate(refs):
-        for f in range((ref.shape[0] - META) // block):
+    for i, (ref, end) in enumerate(metas(refs, rows)):
+        for f in range((rows - META) // block):
             ids = [ids_ref[i, 0, lane + f].astype(jnp.int32) for lane in (OWNER_AT, DEST_AT)]
-            items.append((ref, f * block, *ids))
+            items.append((ref, end + META - rows + f * block, *ids))
     return items
 
 
-def relay_kernel(*refs, block):
-    held, out_refs, ids_ref, sems = refs[: 1 + FAR], refs[1 + FAR : -2], refs[-2], refs[-1]
-    fetch_ids(metas(held), ids_ref, sems)()
+def join_kernel(first_ref, second_ref, out_ref):
+    rows = first_ref.shape[0]
+    out_ref[:rows, :] = first_ref[...]
+    out_ref[rows:, :] = second_ref[...]
+
+
+def relay_kernel(*refs, rows, block):
+    held, out_refs, ids_ref, sems = refs[:2], refs[2:-2], refs[-2], refs[-1]
+    fetch_ids(metas(held, rows), ids_ref, sems)()
     me = lax.axis_index("pitch")
     count = lax.axis_size("pitch")
-    halo = held[0][held[0].shape[0] - META :, :]
-    items = blocks_of(held, block, ids_ref)
+    halo = held[0][rows - META : rows, :]
+    items = blocks_of(held, rows, block, ids_ref)
     targets = [lax.rem(me + count + by, count) for by in near_hops(me)]
     route(items, targets, halo, block, out_refs)
 
@@ -190,9 +193,9 @@
         out_ref[v, :, to] += ref[pl.ds(pl.multiple_of(at + v * ROWS, ROWS), ROWS), :]
 
 
-def base_kernel(flow_ref, speed_ref, first_ref, second_ref, *refs):
-    held, out_ref, ids_ref, sems = refs[: 1 + FAR], refs[-3], refs[-2], refs[-1]
-    wait = fetch_ids(metas(held), ids_ref, sems)
+def base_kernel(flow_ref, speed_ref, first_ref, second_ref, *refs, rows):
+    held, out_ref, ids_ref, sems = refs[:2], refs[-3], refs[-2], refs[-1]
+    wait = fetch_ids(metas(held, rows), ids_ref, sems)
     nvars, _, cells = flow_ref.shape
     block = nvars * ROWS
     per = cells // LANES
@@ -213,7 +216,7 @@
             speed = speed_ref[c : c + 1, :]
             out_ref[v, :, c * LANES : (c + 1) * LANES] = -speed * (up - down) * 0.5
     wait()
-    items = blocks_of(held, block, ids_ref)
+    items = blocks_of(held, rows, block, ids_ref)
     for ref, at, owner, dest in items:
 
         @pl.when(owner == me)
@@ -308,21 +311,24 @@
         flops=6 * 2 * count * count * slots * LANES,
         moved=1_000_000,
     )(by_cell)
-    held = [mine] + [sent_by(mine, far_hops, i) for i in range(FAR)]
+    rows = mine.shape[0]
+    both = call(join_kernel, f32(2 * rows, LANES), [vmem()] * 2, flops=SLOW, moved=500_000)(mine, sent_by(mine, far_hops, 0))
+    held = [both, sent_by(both, far_hops, 1)]
+    planes = 2 * len(held)
     relays = call(
-        functools.partial(relay_kernel, block=block),
-        [f32(len(held) * CAP * block + META, LANES) for _ in range(NEAR)],
+        functools.partial(relay_kernel, rows=rows, block=block),
+        [f32(planes * CAP * block + META, LANES) for _ in range(NEAR)],
         [vmem()] * len(held),
-        id_scratch(len(held)),
+        id_scratch(planes),
         flops=20000000000,
         moved=1_500_000,
     )(*held)
     sent = [sent_by(a, near_hops, i) for i, a in enumerate(relays)]
     base = call(
-        base_kernel,
+        functools.partial(base_kernel, rows=rows),
         f32(nvars, inst, cells),
         [vmem()] * (4 + len(held)),
-        id_scratch(len(held)),
+        id_scratch(planes),
         moved=900_000,
     )(flow, speed, sent[0], sent[1], *held)
 

time: 61.4 us -> 58.4 us (0.951)
  the two profiles are of different devices: /device:TPU:34 before, /device:TPU:2 now
where the time goes in v6:
time: 58.4 us; the launch traced here: 57.9 us
  starting transfers between devices  44.5 us (76%)
  Pallas kernels  7.2 us (12%)
  waiting for transfers between devices  5.41 us (9%)
  between operations  0.78 us (1%)
    ppermute x5, starting transfers between devices, sent_by(): lax.ppermute(array, 'pitch', [(p, (p + hops(p)[i]) % count) for p in rang...  29.1 us
    all_to_all x1, starting transfers between devices, per_device(): by_cell = lax.all_to_all(packed, 'tm', 0, 0, tiled=True)  7.76 us
    all_to_all x1, starting transfers between devices, per_device(): by_time = lax.all_to_all(product, 'tm', 0, 0, tiled=True)  7.62 us
    ppermute x5, waiting for transfers between devices, sent_by(): lax.ppermute(array, 'pitch', [(p, (p + hops(p)[i]) % count) for p in rang...  5.4 us
    pallas_call x1, Pallas kernels, per_device(): call(prepare_kernel, (f32(devs * slots * ROWS, LANES), f32(faces * block...  1.91 us
    pallas_call x1, Pallas kernels, per_device(): call(finish_kernel, (f32(nvars, inst, cells), f32(nvars, cells)), [vmem()...  1.56 us
    pallas_call x1, Pallas kernels, per_device(): call(functools.partial(spectral_kernel, count=count, first_mean=tiles, la...  1.43 us
  transfers between devices with their start and end apart: 7, of which 2 were waited for; matrix products, arithmetic and copies ran while one was open for 0% of the time, Pallas kernels for 6%

profile of v6, /device:TPU:2, one launch (start us, length us, event | category | flops | bytes accessed | tf_op | source)
XLA Modules:
  0.0 57.9 jit_solution(8498404782039341398)
XLA Ops:
  0.6 1.9 %shard_map.77 = (f32[768,128]{1,0:T(8,128)}, f32[168,128]{1,0:T(8,128)}) custom-call(f32[5,8,2048]{2,1,0:T(8,128)} %flow_ref.1, f32[160,128]{1,0:T(8,128)} %bitcast.15, s32[1,4]{1,0:T(1,128)} %bitcast.16, s32[1,4]{1,0:T(1,128)} %bitcast.17, f32[1,4]{1,0:T(1,128)} %bitcast.18), custom_call_target="tpu_custom_call" | custom-call | bytes 1200000 | tf_op jit(solution)/shard_map/pallas_call | solution.py:298
  2.5 9.1 %collective-permute-start = (f32[168,128]{1,0:T(8,128)}, f32[168,128]{1,0:T(8,128)S(1)}, u32[]{:S(2)}, u32[]{:S(2)}) collective-permute-start(f32[168,128]{1,0:T(8,128)} %get-tuple-element.7.first_ref), channel_id=1, source_target_pairs={{0,4},{1,13},{2,6},{3,15},{4,0},{5,9},{6,2},{7,11},{8,12},{9,5},{1... | collective-permute-start | bytes 258056 | tf_op jit(solution)/shard_map/ppermute | solution.py:282
  11.7 0.0 copy-start.2
  11.7 7.8 %all-to-all-start = ((f32[32,24,128]{2,1,0:T(8,128)}), f32[32,24,128]{2,1,0:T(8,128)S(1)}, u32[]{:S(2)}, u32[]{:S(2)}) async-start(f32[32,24,128]{2,1,0:T(8,128)} %bitcast.14), calls=%async_computation | async-start | bytes 786432 | tf_op jit(solution)/shard_map/all_to_all | solution.py:306
  19.4 0.0 collective-permute-done.second_ref
  19.4 0.0 copy-done.2
  19.5 9.6 %collective-permute-start.1 = (f32[336,128]{1,0:T(8,128)S(1)}, f32[336,128]{1,0:T(8,128)S(1)}, u32[]{:S(2)}, u32[]{:S(2)}) collective-permute-start(f32[336,128]{1,0:T(8,128)S(1)} %shard_map.78.refs_0_), channel_id=1, source_target_pairs={{0,12},{1,5},{2,14},{3,7},{4,8},{5,1},{6,10},{7,3},{8,4},{9,13},{1... | collective-permute-start | bytes 516104 | tf_op jit(solution)/shard_map/ppermute | solution.py:282
  29.1 0.0 all-to-all-done
  29.1 1.4 %shard_map.81 = f32[768,128]{1,0:T(8,128)} custom-call(f32[768,128]{1,0:T(8,128)S(1)} %bitcast.12), custom_call_target="tpu_custom_call" | custom-call | flops 301989888 | bytes 1000000 | tf_op jit(solution)/shard_map/pallas_call | solution.py:307
  30.6 7.6 %all-to-all-start.1 = ((f32[32,24,128]{2,1,0:T(8,128)}), f32[32,24,128]{2,1,0:T(8,128)S(1)}, u32[]{:S(2)}, u32[]{:S(2)}) async-start(f32[32,24,128]{2,1,0:T(8,128)} %bitcast.8), calls=%async_computation.1 | async-start | bytes 786432 | tf_op jit(solution)/shard_map/all_to_all | solution.py:335
  38.2 0.0 copy-start
  38.2 2.4 %collective-permute-done.1.refs_1_ = f32[336,128]{1,0:T(8,128)S(1)} collective-permute-done((f32[336,128]{1,0:T(8,128)S(1)}, f32[336,128]{1,0:T(8,128)S(1)}, u32[]{:S(2)}, u32[]{:S(2)}) %collective-permute-start.1) | collective-permute-done | bytes 172064 | tf_op jit(solution)/shard_map/ppermute | solution.py:282
  40.6 0.0 copy-start.1
  40.6 1.1 %shard_map.79 = (f32[328,128]{1,0:T(8,128)S(1)}, f32[328,128]{1,0:T(8,128)S(1)}, f32[328,128]{1,0:T(8,128)S(1)}) custom-call(f32[336,128]{1,0:T(8,128)S(1)} %shard_map.78.refs_0_, f32[336,128]{1,0:T(8,128)S(1)} %collective-permute-done.1.refs_1_), custom_call_target="tpu_custom_call" | custom-call | flops 20000000000 | bytes 1500000 | tf_op jit(solution)/shard_map/pallas_call | solution.py:318
  41.8 1.9 %collective-permute-start.2 = (f32[328,128]{1,0:T(8,128)S(1)}, f32[328,128]{1,0:T(8,128)S(1)}, u32[]{:S(2)}, u32[]{:S(2)}) collective-permute-start(f32[328,128]{1,0:T(8,128)S(1)} %get-tuple-element.8), channel_id=1, source_target_pairs={{0,15},{1,2},{2,1},{3,4},{4,3},{5,6},{6,5},{7,8},{8,7},{9,10},{10,... | collective-permute-start | bytes 503816 | tf_op jit(solution)/shard_map/ppermute | solution.py:282
  43.7 1.9 %collective-permute-start.3 = (f32[328,128]{1,0:T(8,128)S(1)}, f32[328,128]{1,0:T(8,128)S(1)}, u32[]{:S(2)}, u32[]{:S(2)}) collective-permute-start(f32[328,128]{1,0:T(8,128)S(1)} %get-tuple-element.9), channel_id=1, source_target_pairs={{0,1},{1,0},{2,3},{3,2},{4,5},{5,4},{6,7},{7,6},{8,9},{9,8},{10,11... | collective-permute-start | bytes 503816 | tf_op jit(solution)/shard_map/ppermute | solution.py:282
  45.6 6.6 %collective-permute-start.4 = (f32[328,128]{1,0:T(8,128)S(1)}, f32[328,128]{1,0:T(8,128)S(1)}, u32[]{:S(2)}, u32[]{:S(2)}) collective-permute-start(f32[328,128]{1,0:T(8,128)S(1)} %get-tuple-element.11), channel_id=1, source_target_pairs={{0,14},{1,3},{2,0},{3,5},{4,2},{5,7},{6,4},{7,9},{8,6},{9,11},{10,... | collective-permute-start | bytes 503816 | tf_op jit(solution)/shard_map/ppermute | solution.py:282
  52.2 0.0 collective-permute-done.2.first_ref.refs_2_
  52.2 3.0 %collective-permute-done.3.second_ref.refs_3_ = f32[328,128]{1,0:T(8,128)S(1)} collective-permute-done((f32[328,128]{1,0:T(8,128)S(1)}, f32[328,128]{1,0:T(8,128)S(1)}, u32[]{:S(2)}, u32[]{:S(2)}) %collective-permute-start.3) | collective-permute-done | bytes 167968 | tf_op jit(solution)/shard_map/ppermute | solution.py:282
  55.2 0.0 copy-done
  55.2 0.0 copy-done.1
  55.2 1.1 %shard_map.80.refs_0_ = f32[5,8,2048]{2,1,0:T(8,128)S(1)} custom-call(f32[5,8,2048]{2,1,0:T(8,128)S(1)} %copy-done, f32[16,128]{1,0:T(8,128)S(1)} %bitcast.13, f32[328,128]{1,0:T(8,128)S(1)} %collective-permute-done.2.first_ref.refs_2_, f32[328,128]{1,0:T(8,128)S(1)} %collective-permute-done.3.second_ref.refs_3_, f32[336,128]{1,0:T(8,128)S(1)} %shard_map.78.refs_0_, ...), custom_call_target="tpu_custom_call" | custom-call | bytes 900000 | tf_op jit(solution)/shard_map/pallas_call | solution.py:327
  56.4 0.0 collective-permute-done.4.refs_4_
  56.4 0.0 all-to-all-done.1
  56.4 1.6 %shard_map.82 = (f32[5,8,2048]{2,1,0:T(8,128)}, f32[5,2048]{1,0:T(8,128)}) custom-call(f32[5,8,2048]{2,1,0:T(8,128)S(1)} %shard_map.80.refs_0_, f32[768,128]{1,0:T(8,128)S(1)} %bitcast.11, f32[328,128]{1,0:T(8,128)S(1)} %collective-permute-done.2.first_ref.refs_2_, f32[328,128]{1,0:T(8,128)S(1)} %collective-permute-done.3.second_ref.refs_3_, ...), custom_call_target="tpu_custom_call" | custom-call | bytes 1500000 | tf_op jit(solution)/shard_map/pallas_call | solution.py:336
  (1 shorter events, 0.0 us)
Async XLA Ops:
  2.5 16.9 %collective-permute-start = (f32[168,128]{1,0:T(8,128)}, f32[168,128]{1,0:T(8,128)S(1)}, u32[]{:S(2)}, u32[]{:S(2)}) collective-permute-start(f32[168,128]{1,0:T(8,128)} %get-tuple-element.7.first_ref), channel_id=1, source_target_pairs={{0,4},{1,13},{2,6},{3,15},{4,0},{5,9},{6,2},{7,11},{8,12},{9,5},{1... | collective-permute-start | bytes 258056 | tf_op jit(solution)/shard_map/ppermute | solution.py:282
  11.7 7.8 %copy-start.2 = (f32[168,128]{1,0:T(8,128)S(1)}, f32[168,128]{1,0:T(8,128)}, u32[]{:S(2)}) copy-start(f32[168,128]{1,0:T(8,128)} %get-tuple-element.7.first_ref) | copy-start | bytes 258052
  11.7 17.4 %all-to-all-start = ((f32[32,24,128]{2,1,0:T(8,128)}), f32[32,24,128]{2,1,0:T(8,128)S(1)}, u32[]{:S(2)}, u32[]{:S(2)}) async-start(f32[32,24,128]{2,1,0:T(8,128)} %bitcast.14), calls=%async_computation | async-start | bytes 786432 | tf_op jit(solution)/shard_map/all_to_all | solution.py:306
  19.5 21.2 %collective-permute-start.1 = (f32[336,128]{1,0:T(8,128)S(1)}, f32[336,128]{1,0:T(8,128)S(1)}, u32[]{:S(2)}, u32[]{:S(2)}) collective-permute-start(f32[336,128]{1,0:T(8,128)S(1)} %shard_map.78.refs_0_), channel_id=1, source_target_pairs={{0,12},{1,5},{2,14},{3,7},{4,8},{5,1},{6,10},{7,3},{8,4},{9,13},{1... | collective-permute-start | bytes 516104 | tf_op jit(solution)/shard_map/ppermute | solution.py:282
  30.6 25.8 %all-to-all-start.1 = ((f32[32,24,128]{2,1,0:T(8,128)}), f32[32,24,128]{2,1,0:T(8,128)S(1)}, u32[]{:S(2)}, u32[]{:S(2)}) async-start(f32[32,24,128]{2,1,0:T(8,128)} %bitcast.8), calls=%async_computation.1 | async-start | bytes 786432 | tf_op jit(solution)/shard_map/all_to_all | solution.py:335
  38.2 17.0 %copy-start = (f32[5,8,2048]{2,1,0:T(8,128)S(1)}, f32[5,8,2048]{2,1,0:T(8,128)}, u32[]{:S(2)}) copy-start(f32[5,8,2048]{2,1,0:T(8,128)} %flow_ref.1) | copy-start | bytes 983044
  40.6 14.6 %copy-start.1 = (f32[2048]{0:T(1024)S(1)}, f32[2048]{0:T(1024)}, u32[]{:S(2)}) copy-start(f32[2048]{0:T(1024)} %param.7) | copy-start | bytes 24580
  41.8 10.5 %collective-permute-start.2 = (f32[328,128]{1,0:T(8,128)S(1)}, f32[328,128]{1,0:T(8,128)S(1)}, u32[]{:S(2)}, u32[]{:S(2)}) collective-permute-start(f32[328,128]{1,0:T(8,128)S(1)} %get-tuple-element.8), channel_id=1, source_target_pairs={{0,15},{1,2},{2,1},{3,4},{4,3},{5,6},{6,5},{7,8},{8,7},{9,10},{10,... | collective-permute-start | bytes 503816 | tf_op jit(solution)/shard_map/ppermute | solution.py:282
  43.7 11.5 %collective-permute-start.3 = (f32[328,128]{1,0:T(8,128)S(1)}, f32[328,128]{1,0:T(8,128)S(1)}, u32[]{:S(2)}, u32[]{:S(2)}) collective-permute-start(f32[328,128]{1,0:T(8,128)S(1)} %get-tuple-element.9), channel_id=1, source_target_pairs={{0,1},{1,0},{2,3},{3,2},{4,5},{5,4},{6,7},{7,6},{8,9},{9,8},{10,11... | collective-permute-start | bytes 503816 | tf_op jit(solution)/shard_map/ppermute | solution.py:282
  45.6 10.7 %collective-permute-start.4 = (f32[328,128]{1,0:T(8,128)S(1)}, f32[328,128]{1,0:T(8,128)S(1)}, u32[]{:S(2)}, u32[]{:S(2)}) collective-permute-start(f32[328,128]{1,0:T(8,128)S(1)} %get-tuple-element.11), channel_id=1, source_target_pairs={{0,14},{1,3},{2,0},{3,5},{4,2},{5,7},{6,4},{7,9},{8,6},{9,11},{10,... | collective-permute-start | bytes 503816 | tf_op jit(solution)/shard_map/ppermute | solution.py:282

commit v7 on v6

--- a/solution.py
+++ b/solution.py
@@ -193,35 +193,32 @@
         out_ref[v, :, to] += ref[pl.ds(pl.multiple_of(at + v * ROWS, ROWS), ROWS), :]
 
 
-def base_kernel(flow_ref, speed_ref, first_ref, second_ref, *refs, rows):
-    held, out_ref, ids_ref, sems = refs[:2], refs[-3], refs[-2], refs[-1]
-    wait = fetch_ids(metas(held, rows), ids_ref, sems)
+def base_kernel(flow_ref, speed_ref, out_ref):
     nvars, _, cells = flow_ref.shape
-    block = nvars * ROWS
     per = cells // LANES
-    me = lax.axis_index("pitch")
     lane = lax.broadcasted_iota(jnp.int32, (ROWS, LANES), 1)
-    first, second = [ref[ref.shape[0] - META :, :] for ref in (first_ref, second_ref)]
-    odd = lax.rem(me, 2) == 1
-    before, after = jnp.where(odd, second, first), jnp.where(odd, first, second)
+    edge = jnp.zeros((ROWS, LANES), jnp.float32)
     for v in range(nvars):
-        left_edge = pltpu.roll(before, (LANES - v) % LANES, 1)
-        right_edge = pltpu.roll(after, LANES - 1 - nvars - v, 1)
         tiles = [flow_ref[v, :, c * LANES : (c + 1) * LANES] for c in range(per)]
         downs = [pltpu.roll(tile, 1, 1) for tile in tiles]
         ups = [pltpu.roll(tile, LANES - 1, 1) for tile in tiles]
         for c in range(per):
-            down = jnp.where(lane == 0, left_edge if c == 0 else downs[c - 1], downs[c])
-            up = jnp.where(lane == LANES - 1, right_edge if c == per - 1 else ups[c + 1], ups[c])
-            speed = speed_ref[c : c + 1, :]
-            out_ref[v, :, c * LANES : (c + 1) * LANES] = -speed * (up - down) * 0.5
-    wait()
-    items = blocks_of(held, rows, block, ids_ref)
-    for ref, at, owner, dest in items:
-
-        @pl.when(owner == me)
-        def _(ref=ref, at=at, dest=dest):
-            add_block(out_ref, ref, at, dest)
+            down = jnp.where(lane == 0, edge if c == 0 else downs[c - 1], downs[c])
+            up = jnp.where(lane == LANES - 1, edge if c == per - 1 else ups[c + 1], ups[c])
+            out_ref[v, :, c * LANES : (c + 1) * LANES] = -speed_ref[c : c + 1, :] * (up - down) * 0.5
+
+
+def add_edges(out_ref, speed_ref, first, second):
+    nvars, _, cells = out_ref.shape
+    lane = lax.broadcasted_iota(jnp.int32, (ROWS, LANES), 1)
+    odd = lax.rem(lax.axis_index("pitch"), 2) == 1
+    before, after = jnp.where(odd, second, first), jnp.where(odd, first, second)
+    last = cells // LANES - 1
+    for v in range(nvars):
+        left = pltpu.roll(before, (LANES - v) % LANES, 1)
+        right = pltpu.roll(after, LANES - 1 - nvars - v, 1)
+        out_ref[v, :, :LANES] += jnp.where(lane == 0, speed_ref[:1, :] * left * 0.5, 0.0)
+        out_ref[v, :, cells - LANES :] += jnp.where(lane == LANES - 1, -speed_ref[last:, :] * right * 0.5, 0.0)
 
 
 def spectral_matrix(count):
@@ -254,10 +251,10 @@
             out_ref[at : at + ROWS, :] = jnp.where(is_mean, mean, part)
 
 
-def finish_kernel(*refs):
-    base_ref, cells_ref, blocks = refs[0], refs[1], refs[2:-4]
+def finish_kernel(*refs, rows):
+    base_ref, cells_ref, speed_ref, held, blocks = refs[0], refs[1], refs[2], refs[3:5], refs[5:-4]
     out_ref, mean_ref, ids_ref, sems = refs[-4:]
-    wait = fetch_ids(metas(blocks), ids_ref, sems)
+    wait = fetch_ids(metas(blocks) + metas(held, rows), ids_ref, sems)
     nvars, _, cells = out_ref.shape
     block = nvars * ROWS
     per = cells // LANES
@@ -267,7 +264,15 @@
         out_ref[v, :, at] = cells_ref[m * ROWS : (m + 1) * ROWS, :] + base_ref[v, :, at]
         row = nvars * per * ROWS + m
         mean_ref[v : v + 1, at] = cells_ref[row : row + 1, :]
+    add_edges(out_ref, speed_ref, *[ref[ref.shape[0] - META :, :] for ref in blocks[:2]])
     wait()
+    me = lax.axis_index("pitch")
+    for ref, at, owner, dest in blocks_of(held, rows, block, ids_ref.at[pl.ds(NEAR, ids_ref.shape[0] - NEAR)]):
+
+        @pl.when(owner == me)
+        def _(ref=ref, at=at, dest=dest):
+            add_block(out_ref, ref, at, dest)
+
     for i, ref in enumerate(blocks):
 
         def add(slot, carry, i=i, ref=ref):
@@ -324,22 +329,15 @@
         moved=1_500_000,
     )(*held)
     sent = [sent_by(a, near_hops, i) for i, a in enumerate(relays)]
-    base = call(
-        functools.partial(base_kernel, rows=rows),
-        f32(nvars, inst, cells),
-        [vmem()] * (4 + len(held)),
-        id_scratch(planes),
-        moved=900_000,
-    )(flow, speed, sent[0], sent[1], *held)
-
+    base = call(base_kernel, f32(nvars, inst, cells), [vmem()] * 2, moved=900_000)(flow, speed)
     by_time = lax.all_to_all(product, "tm", 0, 0, tiled=True)
     residual, mean_flow = call(
-        finish_kernel,
+        functools.partial(finish_kernel, rows=rows),
         (f32(nvars, inst, cells), f32(nvars, cells)),
-        [vmem()] * (2 + len(sent)),
-        id_scratch(len(sent)),
+        [vmem()] * (5 + len(sent)),
+        id_scratch(planes + len(sent)),
         moved=1_500_000,
-    )(base, by_time, *sent)
+    )(base, by_time, speed, *held, *sent)
     return residual, mean_flow
 
 

time: 58.4 us -> 58 us (level)
  the two profiles are of different devices: /device:TPU:2 before, /device:TPU:34 now
where the time goes in v7:
time: 58 us; the launch traced here: 57.6 us
  starting transfers between devices  40.1 us (69%)
  waiting for transfers between devices  9.86 us (17%)
  Pallas kernels  6.79 us (12%)
  between operations  0.79 us (1%)
    ppermute x5, starting transfers between devices, sent_by(): lax.ppermute(array, 'pitch', [(p, (p + hops(p)[i]) % count) for p in rang...  27.2 us
    all_to_all x1, starting transfers between devices, per_device(): by_cell = lax.all_to_all(packed, 'tm', 0, 0, tiled=True)  7.76 us
    ppermute x5, waiting for transfers between devices, sent_by(): lax.ppermute(array, 'pitch', [(p, (p + hops(p)[i]) % count) for p in rang...  6.65 us
    all_to_all x1, starting transfers between devices, per_device(): by_time = lax.all_to_all(product, 'tm', 0, 0, tiled=True)  5.12 us
    all_to_all x1, waiting for transfers between devices, per_device(): by_cell = lax.all_to_all(packed, 'tm', 0, 0, tiled=True)  3.21 us
    pallas_call x1, Pallas kernels, per_device(): call(functools.partial(finish_kernel, rows=rows), (f32(nvars, inst, cells...  2.06 us
    pallas_call x1, Pallas kernels, per_device(): call(prepare_kernel, (f32(devs * slots * ROWS, LANES), f32(faces * block...  1.91 us
    pallas_call x1, Pallas kernels, per_device(): call(functools.partial(spectral_kernel, count=count, first_mean=tiles, la...  1.43 us
  transfers between devices with their start and end apart: 7, of which 3 were waited for; matrix products, arithmetic and copies ran while one was open for 0% of the time, Pallas kernels for 5%

profile of v7, /device:TPU:34, one launch (start us, length us, event | category | flops | bytes accessed | tf_op | source)
XLA Modules:
  0.0 57.6 jit_solution(7601520867612389745)
XLA Ops:
  0.6 1.9 %shard_map.78 = (f32[768,128]{1,0:T(8,128)}, f32[168,128]{1,0:T(8,128)}) custom-call(f32[5,8,2048]{2,1,0:T(8,128)} %refs_0_.1, f32[160,128]{1,0:T(8,128)} %bitcast.16, s32[1,4]{1,0:T(1,128)} %bitcast.17, s32[1,4]{1,0:T(1,128)} %bitcast.18, f32[1,4]{1,0:T(1,128)} %bitcast.19), custom_call_target="tpu_custom_call" | custom-call | bytes 1200000 | tf_op jit(solution)/shard_map/pallas_call | solution.py:303
  2.5 11.8 %collective-permute-start = (f32[168,128]{1,0:T(8,128)}, f32[168,128]{1,0:T(8,128)S(1)}, u32[]{:S(2)}, u32[]{:S(2)}) collective-permute-start(f32[168,128]{1,0:T(8,128)} %get-tuple-element.8.first_ref), channel_id=1, source_target_pairs={{0,4},{1,13},{2,6},{3,15},{4,0},{5,9},{6,2},{7,11},{8,12},{9,5},{1... | collective-permute-start | bytes 258056 | tf_op jit(solution)/shard_map/ppermute | solution.py:287
  14.4 0.0 copy-start.2
  14.4 7.8 %all-to-all-start = ((f32[32,24,128]{2,1,0:T(8,128)}), f32[32,24,128]{2,1,0:T(8,128)S(1)}, u32[]{:S(2)}, u32[]{:S(2)}) async-start(f32[32,24,128]{2,1,0:T(8,128)} %bitcast.15), calls=%async_computation | async-start | bytes 786432 | tf_op jit(solution)/shard_map/all_to_all | solution.py:311
  22.2 0.0 collective-permute-done.second_ref
  22.2 0.0 copy-done.2
  22.2 5.5 %collective-permute-start.1 = (f32[336,128]{1,0:T(8,128)S(1)}, f32[336,128]{1,0:T(8,128)S(1)}, u32[]{:S(2)}, u32[]{:S(2)}) collective-permute-start(f32[336,128]{1,0:T(8,128)S(1)} %shard_map.80.refs_0_.refs_3_), channel_id=1, source_target_pairs={{0,12},{1,5},{2,14},{3,7},{4,8},{5,1},{6,10},{7,3},{8,4},{9,13},{1... | collective-permute-start | bytes 516104 | tf_op jit(solution)/shard_map/ppermute | solution.py:287
  27.7 3.2 %all-to-all-done = f32[32,24,128]{2,1,0:T(8,128)S(1)} async-done(((f32[32,24,128]{2,1,0:T(8,128)}), f32[32,24,128]{2,1,0:T(8,128)S(1)}, u32[]{:S(2)}, u32[]{:S(2)}) %all-to-all-start) | async-done | bytes 393248 | tf_op jit(solution)/shard_map/all_to_all | solution.py:311
  30.9 1.4 %shard_map.79 = f32[768,128]{1,0:T(8,128)} custom-call(f32[768,128]{1,0:T(8,128)S(1)} %bitcast.12), custom_call_target="tpu_custom_call" | custom-call | flops 301989888 | bytes 1000000 | tf_op jit(solution)/shard_map/pallas_call | solution.py:312
  32.3 5.1 %all-to-all-start.1 = ((f32[32,24,128]{2,1,0:T(8,128)}), f32[32,24,128]{2,1,0:T(8,128)S(1)}, u32[]{:S(2)}, u32[]{:S(2)}) async-start(f32[32,24,128]{2,1,0:T(8,128)} %bitcast.8), calls=%async_computation.1 | async-start | bytes 786432 | tf_op jit(solution)/shard_map/all_to_all | solution.py:333
  37.5 0.0 copy-start
  37.5 0.0 collective-permute-done.1.refs_1_.refs_4_
  37.5 0.0 copy-start.1
  37.5 1.1 %shard_map.81 = (f32[328,128]{1,0:T(8,128)S(1)}, f32[328,128]{1,0:T(8,128)S(1)}, f32[328,128]{1,0:T(8,128)S(1)}) custom-call(f32[336,128]{1,0:T(8,128)S(1)} %shard_map.80.refs_0_.refs_3_, f32[336,128]{1,0:T(8,128)S(1)} %collective-permute-done.1.refs_1_.refs_4_), custom_call_target="tpu_custom_call" | custom-call | flops 20000000000 | bytes 1500000 | tf_op jit(solution)/shard_map/pallas_call | solution.py:323
  38.6 2.0 %collective-permute-start.2 = (f32[328,128]{1,0:T(8,128)S(1)}, f32[328,128]{1,0:T(8,128)S(1)}, u32[]{:S(2)}, u32[]{:S(2)}) collective-permute-start(f32[328,128]{1,0:T(8,128)S(1)} %get-tuple-element.9), channel_id=1, source_target_pairs={{0,15},{1,2},{2,1},{3,4},{4,3},{5,6},{6,5},{7,8},{8,7},{9,10},{10,... | collective-permute-start | bytes 503816 | tf_op jit(solution)/shard_map/ppermute | solution.py:287
  40.6 5.2 %collective-permute-start.3 = (f32[328,128]{1,0:T(8,128)S(1)}, f32[328,128]{1,0:T(8,128)S(1)}, u32[]{:S(2)}, u32[]{:S(2)}) collective-permute-start(f32[328,128]{1,0:T(8,128)S(1)} %get-tuple-element.10), channel_id=1, source_target_pairs={{0,1},{1,0},{2,3},{3,2},{4,5},{5,4},{6,7},{7,6},{8,9},{9,8},{10,11... | collective-permute-start | bytes 503816 | tf_op jit(solution)/shard_map/ppermute | solution.py:287
  45.8 2.8 %collective-permute-start.4 = (f32[328,128]{1,0:T(8,128)S(1)}, f32[328,128]{1,0:T(8,128)S(1)}, u32[]{:S(2)}, u32[]{:S(2)}) collective-permute-start(f32[328,128]{1,0:T(8,128)S(1)} %get-tuple-element.11), channel_id=1, source_target_pairs={{0,14},{1,3},{2,0},{3,5},{4,2},{5,7},{6,4},{7,9},{8,6},{9,11},{10,... | collective-permute-start | bytes 503816 | tf_op jit(solution)/shard_map/ppermute | solution.py:287
  48.6 0.0 copy-done
  48.6 0.0 copy-done.1
  48.6 0.2 shard_map.77.refs_0_
  48.9 0.0 collective-permute-done.2.refs_5_
  48.9 4.0 %collective-permute-done.3.refs_6_ = f32[328,128]{1,0:T(8,128)S(1)} collective-permute-done((f32[328,128]{1,0:T(8,128)S(1)}, f32[328,128]{1,0:T(8,128)S(1)}, u32[]{:S(2)}, u32[]{:S(2)}) %collective-permute-start.3) | collective-permute-done | bytes 167968 | tf_op jit(solution)/shard_map/ppermute | solution.py:287
  52.9 2.6 %collective-permute-done.4.refs_7_ = f32[328,128]{1,0:T(8,128)S(1)} collective-permute-done((f32[328,128]{1,0:T(8,128)S(1)}, f32[328,128]{1,0:T(8,128)S(1)}, u32[]{:S(2)}, u32[]{:S(2)}) %collective-permute-start.4) | collective-permute-done | bytes 167968 | tf_op jit(solution)/shard_map/ppermute | solution.py:287
  55.5 0.0 all-to-all-done.1
  55.5 2.1 %shard_map.82 = (f32[5,8,2048]{2,1,0:T(8,128)}, f32[5,2048]{1,0:T(8,128)}) custom-call(f32[5,8,2048]{2,1,0:T(8,128)S(1)} %shard_map.77.refs_0_, f32[768,128]{1,0:T(8,128)S(1)} %bitcast.11, f32[16,128]{1,0:T(8,128)S(1)} %bitcast.14, f32[336,128]{1,0:T(8,128)S(1)} %shard_map.80.refs_0_.refs_3_, f32[336,128]{1,0:T(8,128)S(1)} %collective-permute-done.1.refs_1_.refs_4_, ...), custom_call_target="tpu_custom_call" | custom-call | bytes 1500000 | tf_op jit(solution)/shard_map/pallas_call | solution.py:334
  (1 shorter events, 0.0 us)
Async XLA Ops:
  2.5 19.6 %collective-permute-start = (f32[168,128]{1,0:T(8,128)}, f32[168,128]{1,0:T(8,128)S(1)}, u32[]{:S(2)}, u32[]{:S(2)}) collective-permute-start(f32[168,128]{1,0:T(8,128)} %get-tuple-element.8.first_ref), channel_id=1, source_target_pairs={{0,4},{1,13},{2,6},{3,15},{4,0},{5,9},{6,2},{7,11},{8,12},{9,5},{1... | collective-permute-start | bytes 258056 | tf_op jit(solution)/shard_map/ppermute | solution.py:287
  14.4 7.8 %copy-start.2 = (f32[168,128]{1,0:T(8,128)S(1)}, f32[168,128]{1,0:T(8,128)}, u32[]{:S(2)}) copy-start(f32[168,128]{1,0:T(8,128)} %get-tuple-element.8.first_ref) | copy-start | bytes 258052
  14.4 16.5 %all-to-all-start = ((f32[32,24,128]{2,1,0:T(8,128)}), f32[32,24,128]{2,1,0:T(8,128)S(1)}, u32[]{:S(2)}, u32[]{:S(2)}) async-start(f32[32,24,128]{2,1,0:T(8,128)} %bitcast.15), calls=%async_computation | async-start | bytes 786432 | tf_op jit(solution)/shard_map/all_to_all | solution.py:311
  22.2 15.3 %collective-permute-start.1 = (f32[336,128]{1,0:T(8,128)S(1)}, f32[336,128]{1,0:T(8,128)S(1)}, u32[]{:S(2)}, u32[]{:S(2)}) collective-permute-start(f32[336,128]{1,0:T(8,128)S(1)} %shard_map.80.refs_0_.refs_3_), channel_id=1, source_target_pairs={{0,12},{1,5},{2,14},{3,7},{4,8},{5,1},{6,10},{7,3},{8,4},{9,13},{1... | collective-permute-start | bytes 516104 | tf_op jit(solution)/shard_map/ppermute | solution.py:287
  32.3 23.2 %all-to-all-start.1 = ((f32[32,24,128]{2,1,0:T(8,128)}), f32[32,24,128]{2,1,0:T(8,128)S(1)}, u32[]{:S(2)}, u32[]{:S(2)}) async-start(f32[32,24,128]{2,1,0:T(8,128)} %bitcast.8), calls=%async_computation.1 | async-start | bytes 786432 | tf_op jit(solution)/shard_map/all_to_all | solution.py:333
  37.5 11.1 %copy-start = (f32[5,8,2048]{2,1,0:T(8,128)S(1)}, f32[5,8,2048]{2,1,0:T(8,128)}, u32[]{:S(2)}) copy-start(f32[5,8,2048]{2,1,0:T(8,128)} %refs_0_.1) | copy-start | bytes 983044
  37.5 11.1 %copy-start.1 = (f32[2048]{0:T(1024)S(1)}, f32[2048]{0:T(1024)}, u32[]{:S(2)}) copy-start(f32[2048]{0:T(1024)} %param.7) | copy-start | bytes 24580
  38.6 10.2 %collective-permute-start.2 = (f32[328,128]{1,0:T(8,128)S(1)}, f32[328,128]{1,0:T(8,128)S(1)}, u32[]{:S(2)}, u32[]{:S(2)}) collective-permute-start(f32[328,128]{1,0:T(8,128)S(1)} %get-tuple-element.9), channel_id=1, source_target_pairs={{0,15},{1,2},{2,1},{3,4},{4,3},{5,6},{6,5},{7,8},{8,7},{9,10},{10,... | collective-permute-start | bytes 503816 | tf_op jit(solution)/shard_map/ppermute | solution.py:287
  40.6 12.3 %collective-permute-start.3 = (f32[328,128]{1,0:T(8,128)S(1)}, f32[328,128]{1,0:T(8,128)S(1)}, u32[]{:S(2)}, u32[]{:S(2)}) collective-permute-start(f32[328,128]{1,0:T(8,128)S(1)} %get-tuple-element.10), channel_id=1, source_target_pairs={{0,1},{1,0},{2,3},{3,2},{4,5},{5,4},{6,7},{7,6},{8,9},{9,8},{10,11... | collective-permute-start | bytes 503816 | tf_op jit(solution)/shard_map/ppermute | solution.py:287
  45.8 9.7 %collective-permute-start.4 = (f32[328,128]{1,0:T(8,128)S(1)}, f32[328,128]{1,0:T(8,128)S(1)}, u32[]{:S(2)}, u32[]{:S(2)}) collective-permute-start(f32[328,128]{1,0:T(8,128)S(1)} %get-tuple-element.11), channel_id=1, source_target_pairs={{0,14},{1,3},{2,0},{3,5},{4,2},{5,7},{6,4},{7,9},{8,6},{9,11},{10,... | collective-permute-start | bytes 503816 | tf_op jit(solution)/shard_map/ppermute | solution.py:287
